TPU v7x, 128 devices: a whole 4x4x4 slice. The times are simulated.
128 devices in a mesh: expert: 32 (over z, x, core), tensor: 4 (over y).
Axes of the slice: x: 4, y: 4, z: 4, core: 2. Of those that a mesh axis runs over, the one named last changes fastest.
Arguments:
- tokens: bfloat16 [8192, 2048], P('expert'), may hold values from -6 to 6
- cotangent: bfloat16 [8192, 2048], P('expert'), may hold values from -6 to 6
- attn_gain: float32 [2048], replicated, may hold values from 0.5 to 1.5
- w_query: bfloat16 [2048, 3072], P(None, 'tensor'), may hold values from -0.125 to 0.125
- w_latent: bfloat16 [2048, 576], replicated, may hold values from -0.125 to 0.125
- latent_gain: float32 [512], replicated, may hold values from 0.5 to 1.5
- w_keyvalue: bfloat16 [512, 4096], P(None, 'tensor'), may hold values from -0.25 to 0.25
- w_output: bfloat16 [2048, 2048], P('tensor'), may hold values from -0.75 to 0.75
- ffn_gain: float32 [2048], replicated, may hold values from 0.5 to 1.5
- w_router: bfloat16 [2048, 64], replicated, may hold values from -0.0625 to 0.0625
- shared_gate: bfloat16 [2048, 2816], P(None, 'tensor'), may hold values from -0.125 to 0.125
- shared_up: bfloat16 [2048, 2816], P(None, 'tensor'), may hold values from -0.125 to 0.125
- shared_down: bfloat16 [2816, 2048], P('tensor'), may hold values from -0.109375 to 0.109375
- expert_gate: bfloat16 [64, 2048, 1408], P('expert', None, 'tensor'), may hold values from -0.125 to 0.125
- expert_up: bfloat16 [64, 2048, 1408], P('expert', None, 'tensor'), may hold values from -0.125 to 0.125
- expert_down: bfloat16 [64, 1408, 2048], P('expert', 'tensor'), may hold values from -0.15625 to 0.15625
- routes: int32 [8192, 6], P('expert'), may hold values from 0 to 63, all different within a row; in each aligned block of 256 rows (0 to 255, 256 to 511, ...) at most 32 rows name the same one
Outputs:
- output: bfloat16 [8192, 2048], P('expert')
- grad_tokens: bfloat16 [8192, 2048], P('expert')
- grad_attn_gain: float32 [2048], P('expert')
- grad_query: float32 [2048, 3072], P('expert', 'tensor')
- grad_latent: float32 [2048, 576], P('expert')
- grad_latent_gain: float32 [512], P('expert')
- grad_keyvalue: float32 [512, 4096], P('expert', 'tensor')
- grad_output: float32 [2048, 2048], P('tensor', 'expert')
- grad_ffn_gain: float32 [2048], P('expert')
- grad_router: float32 [2048, 64], P('expert')
- grad_shared_gate: float32 [2048, 2816], P('expert', 'tensor')
- grad_shared_up: float32 [2048, 2816], P('expert', 'tensor')
- grad_shared_down: float32 [2816, 2048], P('tensor', 'expert')
- grad_expert_gate: float32 [64, 2048, 1408], P('expert', None, 'tensor')
- grad_expert_up: float32 [64, 2048, 1408], P('expert', None, 'tensor')
- grad_expert_down: float32 [64, 1408, 2048], P('expert', 'tensor')
Inputs may be any that keep to these rules, and one draw needn't show every extreme that they name: `routes`: the 6 experts of a token differ. Among the rows of one device no expert is named more than 32 times, a bound that some block reaches.
All inputs are finite; a program needn't handle non-finite values.
Results may differ from a plain program's by a relative error of at most 0.033.
Values may be sent and summed in bfloat16 or wider, within the bound.
No kernel may reach another device: no remote copies, remote signals or barrier semaphores. Data moves between devices by JAX's collectives and lax.ppermute only.
A program may use at most 256 MiB of HBM per device.

v0:
```python
import jax
import jax.numpy as jnp
from jax import lax
from jax.sharding import PartitionSpec as P

NOPE = 128
ROPE = 64
VDIM = 128
KV_RANK = 512


EPS = 1e-06
THETA = 50000.0
ROUTE_SCALE = 2.446
MASKED = -1e30


def rms_scale(values):
    return lax.rsqrt(jnp.mean(values * values, axis=-1, keepdims=True) + EPS)


def rotary_tables(position, table_width):
    frequency = THETA ** (-2.0 * jnp.arange(table_width // 2, dtype=jnp.float32) / table_width)
    angles = position[:, None] * frequency[None, :]
    return (jnp.cos(angles), jnp.sin(angles))


def rotary(values, cosine_table, sine_table):
    half_width = values.shape[-1] // 2
    former = values[..., :half_width]
    latter = values[..., half_width:]
    return jnp.concatenate(
        [former * cosine_table - latter * sine_table, latter * cosine_table + former * sine_table],
        axis=-1,
    )


def unrotary(grads_in, cosine_table, sine_table):
    half_width = grads_in.shape[-1] // 2
    former = grads_in[..., :half_width]
    latter = grads_in[..., half_width:]
    return jnp.concatenate(
        [former * cosine_table + latter * sine_table, latter * cosine_table - former * sine_table],
        axis=-1,
    )


def norm_back(grad_in, unit_rows, row_scale, gain_vec):
    weighted = grad_in * gain_vec
    return row_scale * (
        weighted - unit_rows * jnp.mean(unit_rows * weighted, axis=-1, keepdims=True)
    )


def silu_back(grad_act, gate_pre, up_pre):
    sigma_gate = jax.nn.sigmoid(gate_pre)
    grad_up = grad_act * gate_pre * sigma_gate
    grad_gate = grad_act * up_pre * sigma_gate * (1.0 + gate_pre * (1.0 - sigma_gate))
    return (grad_gate.astype(jnp.bfloat16), grad_up.astype(jnp.bfloat16))


def matmul(left_side, right_side):
    return jnp.dot(left_side, right_side, preferred_element_type=jnp.float32)


def shards(
    tokens,
    cotangent,
    attn_gain,
    w_query,
    w_latent,
    latent_gain,
    w_keyvalue,
    w_output,
    ffn_gain,
    w_router,
    shared_gate,
    shared_up,
    shared_down,
    expert_gate,
    expert_up,
    expert_down,
    routes,
):
    tok_rows = tokens.shape[0]
    model_width = tokens.shape[1]
    top_count = routes.shape[1]
    expert_count = w_router.shape[1]
    local_experts = expert_gate.shape[0]
    capacity = (4 * tok_rows * top_count + 3 * expert_count - 1) // (3 * expert_count)
    qk_width = NOPE + ROPE
    local_heads = w_query.shape[1] // qk_width
    softmax_scale = qk_width ** (-0.5)
    token_float = tokens.astype(jnp.float32)
    scale_one = rms_scale(token_float)
    unit_one = token_float * scale_one
    normed = (unit_one * attn_gain).astype(jnp.bfloat16)
    position = jnp.arange(tok_rows, dtype=jnp.float32)
    cosine_table, sine_table = rotary_tables(position, ROPE)
    cosine_heads = cosine_table[:, None, :]
    sine_heads = sine_table[:, None, :]
    query_pre = matmul(normed, w_query).reshape(tok_rows, local_heads, qk_width)
    query_low = jnp.concatenate(
        [query_pre[..., :NOPE], rotary(query_pre[..., NOPE:], cosine_heads, sine_heads)], axis=-1
    ).astype(jnp.bfloat16)
    latent = matmul(normed, w_latent)
    compressed = latent[:, :KV_RANK]
    scale_latent = rms_scale(compressed)
    unit_latent = compressed * scale_latent
    latent_normed = (unit_latent * latent_gain).astype(jnp.bfloat16)
    key_rope = rotary(latent[:, KV_RANK:], cosine_table, sine_table)
    keyvalue = matmul(latent_normed, w_keyvalue).reshape(tok_rows, local_heads, NOPE + VDIM)
    key_low = jnp.concatenate(
        [
            keyvalue[..., :NOPE],
            jnp.broadcast_to(key_rope[:, None, :], (tok_rows, local_heads, ROPE)),
        ],
        axis=-1,
    ).astype(jnp.bfloat16)
    value_low = keyvalue[..., NOPE:].astype(jnp.bfloat16)
    causal = position[:, None] >= position[None, :]

    def attention_scores():
        raw_scores = (
            jnp.einsum("thd,shd->hts", query_low, key_low, preferred_element_type=jnp.float32)
            * softmax_scale
        )
        return jnp.where(causal[None, :, :], raw_scores, MASKED)

    scores = attention_scores()
    largest = jnp.max(scores, axis=-1, keepdims=True)
    exp_terms = jnp.exp(scores - largest)
    row_total = jnp.sum(exp_terms, axis=-1, keepdims=True)
    log_total = largest + jnp.log(row_total)
    attn_weights = (exp_terms / row_total).astype(jnp.bfloat16)
    attn_mixed = (
        jnp.einsum("hts,shd->thd", attn_weights, value_low, preferred_element_type=jnp.float32)
        .astype(jnp.bfloat16)
        .reshape(tok_rows, local_heads * VDIM)
    )
    attended = lax.psum(matmul(attn_mixed, w_output).astype(jnp.bfloat16), "tensor").astype(
        jnp.float32
    )
    hidden = token_float + attended
    scale_two = rms_scale(hidden)
    unit_two = hidden * scale_two
    normed_two = (unit_two * ffn_gain).astype(jnp.bfloat16)
    logits = matmul(normed_two, w_router)
    selector = routes[:, :, None] == jnp.arange(expert_count, dtype=jnp.int32)[None, None, :]
    select_float = selector.astype(jnp.float32)
    chosen = jnp.sum(select_float * logits[:, None, :], axis=-1)
    sigmas = jax.nn.sigmoid(chosen)
    sigma_total = jnp.sum(sigmas, axis=-1, keepdims=True)
    gate_weights = ROUTE_SCALE * sigmas / sigma_total
    shared_gate_pre = matmul(normed_two, shared_gate)
    shared_up_pre = matmul(normed_two, shared_up)
    shared_act = (jax.nn.silu(shared_gate_pre) * shared_up_pre).astype(jnp.bfloat16)
    shared_part = matmul(shared_act, shared_down)
    select_int = selector.astype(jnp.int32)
    per_token = jnp.sum(select_int, axis=1)
    earlier = jnp.cumsum(per_token, axis=0) - per_token
    slot_index = jnp.sum(earlier[:, None, :] * select_int, axis=-1)
    target = routes * capacity + slot_index
    flat_total = tok_rows * top_count
    source = (
        jnp.full((expert_count * capacity,), flat_total, jnp.int32)
        .at[target.reshape(-1)]
        .set(jnp.arange(flat_total, dtype=jnp.int32))
    )
    padded_rows = jnp.concatenate([normed_two, jnp.zeros((1, model_width), jnp.bfloat16)], axis=0)
    buffer_shape = (lax.axis_size("expert"), local_experts, capacity, model_width)
    outgoing = padded_rows[source // top_count].reshape(buffer_shape)
    arrived = lax.all_to_all(outgoing, "expert", split_axis=0, concat_axis=0, tiled=True)
    gate_pre = jnp.einsum(
        "secd,edh->sech", arrived, expert_gate, preferred_element_type=jnp.float32
    )
    up_pre = jnp.einsum("secd,edh->sech", arrived, expert_up, preferred_element_type=jnp.float32)
    active = (jax.nn.silu(gate_pre) * up_pre).astype(jnp.bfloat16)
    produced = jnp.einsum(
        "sech,ehd->secd", active, expert_down, preferred_element_type=jnp.float32
    ).astype(jnp.bfloat16)
    returned = lax.all_to_all(produced, "expert", split_axis=0, concat_axis=0, tiled=True).reshape(
        -1, model_width
    )
    picked_out = returned[target].astype(jnp.float32)
    routed_part = jnp.sum(gate_weights[:, :, None] * picked_out, axis=1)
    ffn_branch = lax.psum((shared_part + routed_part).astype(jnp.bfloat16), "tensor").astype(
        jnp.float32
    )
    output = (hidden + ffn_branch).astype(jnp.bfloat16)
    grad_out = cotangent.astype(jnp.float32)
    grad_shared_down = matmul(shared_act.T, cotangent)
    grad_shared_act = matmul(cotangent, shared_down.T)
    shared_gate_grad, shared_up_grad = silu_back(grad_shared_act, shared_gate_pre, shared_up_pre)
    grad_shared_gate = matmul(normed_two.T, shared_gate_grad)
    grad_shared_up = matmul(normed_two.T, shared_up_grad)
    norm_part = matmul(shared_gate_grad, shared_gate.T) + matmul(shared_up_grad, shared_up.T)
    piece_grad = (
        (gate_weights[:, :, None] * grad_out[:, None, :])
        .astype(jnp.bfloat16)
        .reshape(flat_total, model_width)
    )
    padded_grad = jnp.concatenate([piece_grad, jnp.zeros((1, model_width), jnp.bfloat16)], axis=0)
    outgoing_grad = padded_grad[source].reshape(buffer_shape)
    grad_arrived = lax.all_to_all(outgoing_grad, "expert", split_axis=0, concat_axis=0, tiled=True)
    grad_active = jnp.einsum(
        "secd,ehd->sech", grad_arrived, expert_down, preferred_element_type=jnp.float32
    )
    grad_expert_down = jnp.einsum(
        "sech,secd->ehd", active, grad_arrived, preferred_element_type=jnp.float32
    )
    expert_gate_grad, expert_up_grad = silu_back(grad_active, gate_pre, up_pre)
    grad_expert_gate = jnp.einsum(
        "secd,sech->edh", arrived, expert_gate_grad, preferred_element_type=jnp.float32
    )
    grad_expert_up = jnp.einsum(
        "secd,sech->edh", arrived, expert_up_grad, preferred_element_type=jnp.float32
    )
    row_grad = jnp.einsum(
        "sech,edh->secd", expert_gate_grad, expert_gate, preferred_element_type=jnp.float32
    )
    row_grad = (
        row_grad
        + jnp.einsum(
            "sech,edh->secd", expert_up_grad, expert_up, preferred_element_type=jnp.float32
        )
    ).astype(jnp.bfloat16)
    grad_returned = lax.all_to_all(
        row_grad, "expert", split_axis=0, concat_axis=0, tiled=True
    ).reshape(-1, model_width)
    norm_part = norm_part + jnp.sum(grad_returned[target].astype(jnp.float32), axis=1)
    gate_grad_part = jnp.sum(grad_out[:, None, :] * picked_out, axis=-1)
    norm_grad, gate_grad = (
        lax.psum(norm_part.astype(jnp.bfloat16), "tensor").astype(jnp.float32),
        lax.psum(gate_grad_part.astype(jnp.bfloat16), "tensor").astype(jnp.float32),
    )
    weighted_sum = jnp.sum(gate_grad * sigmas, axis=-1, keepdims=True)
    sigma_grad = ROUTE_SCALE * (
        gate_grad / sigma_total - weighted_sum / (sigma_total * sigma_total)
    )
    chosen_grad = sigma_grad * sigmas * (1.0 - sigmas)
    logit_grad = jnp.sum(chosen_grad[:, :, None] * select_float, axis=1).astype(jnp.bfloat16)
    grad_router = matmul(normed_two.T, logit_grad)
    norm_grad = norm_grad + matmul(logit_grad, w_router.T)
    grad_ffn_gain = jnp.sum(norm_grad * unit_two, axis=0)
    hidden_grad = grad_out + norm_back(norm_grad, unit_two, scale_two, ffn_gain)
    branch_low = hidden_grad.astype(jnp.bfloat16)
    grad_output = matmul(attn_mixed.T, branch_low)
    mixed_grad = (
        matmul(branch_low, w_output.T).reshape(tok_rows, local_heads, VDIM).astype(jnp.bfloat16)
    )
    weights_full = jnp.exp(attention_scores() - log_total)
    weights_low = weights_full.astype(jnp.bfloat16)
    value_grad = jnp.einsum(
        "hts,thd->shd", weights_low, mixed_grad, preferred_element_type=jnp.float32
    ).astype(jnp.bfloat16)
    prob_grad = jnp.einsum(
        "thd,shd->hts", mixed_grad, value_low, preferred_element_type=jnp.float32
    )
    row_term = jnp.sum(weights_full * prob_grad, axis=-1, keepdims=True)
    score_grad = (weights_full * (prob_grad - row_term)).astype(jnp.bfloat16)
    query_grad = (
        jnp.einsum("hts,shd->thd", score_grad, key_low, preferred_element_type=jnp.float32)
        * softmax_scale
    ).astype(jnp.bfloat16)
    key_grad = (
        jnp.einsum("hts,thd->shd", score_grad, query_low, preferred_element_type=jnp.float32)
        * softmax_scale
    ).astype(jnp.bfloat16)
    query_pre_grad = jnp.concatenate(
        [
            query_grad[..., :NOPE].astype(jnp.float32),
            unrotary(query_grad[..., NOPE:].astype(jnp.float32), cosine_heads, sine_heads),
        ],
        axis=-1,
    )
    query_pre_grad = query_pre_grad.astype(jnp.bfloat16).reshape(tok_rows, local_heads * qk_width)
    grad_query = matmul(normed.T, query_pre_grad)
    normed_part = matmul(query_pre_grad, w_query.T)
    rope_part = jnp.sum(key_grad[..., NOPE:].astype(jnp.float32), axis=1)
    keyvalue_grad = jnp.concatenate([key_grad[..., :NOPE], value_grad], axis=-1).reshape(
        tok_rows, local_heads * (NOPE + VDIM)
    )
    grad_keyvalue = matmul(latent_normed.T, keyvalue_grad)
    latent_part = matmul(keyvalue_grad, w_keyvalue.T)
    normed_grad, latent_normed_grad, rope_grad = (
        lax.psum(normed_part.astype(jnp.bfloat16), "tensor").astype(jnp.float32),
        lax.psum(latent_part.astype(jnp.bfloat16), "tensor").astype(jnp.float32),
        lax.psum(rope_part.astype(jnp.bfloat16), "tensor").astype(jnp.float32),
    )
    grad_latent_gain = jnp.sum(latent_normed_grad * unit_latent, axis=0)
    compressed_grad = norm_back(latent_normed_grad, unit_latent, scale_latent, latent_gain)
    latent_grad = jnp.concatenate(
        [compressed_grad, unrotary(rope_grad, cosine_table, sine_table)], axis=-1
    ).astype(jnp.bfloat16)
    grad_latent = matmul(normed.T, latent_grad)
    normed_grad = normed_grad + matmul(latent_grad, w_latent.T)
    grad_attn_gain = jnp.sum(normed_grad * unit_one, axis=0)
    grad_tokens = (hidden_grad + norm_back(normed_grad, unit_one, scale_one, attn_gain)).astype(
        jnp.bfloat16
    )
    reduced = (
        lax.psum_scatter(
            grad_attn_gain.astype(jnp.bfloat16), "expert", scatter_dimension=0, tiled=True
        ).astype(jnp.float32),
        lax.psum_scatter(
            grad_query.astype(jnp.bfloat16), "expert", scatter_dimension=0, tiled=True
        ).astype(jnp.float32),
        lax.psum_scatter(
            grad_latent.astype(jnp.bfloat16), "expert", scatter_dimension=0, tiled=True
        ).astype(jnp.float32),
        lax.psum_scatter(
            grad_latent_gain.astype(jnp.bfloat16), "expert", scatter_dimension=0, tiled=True
        ).astype(jnp.float32),
        lax.psum_scatter(
            grad_keyvalue.astype(jnp.bfloat16), "expert", scatter_dimension=0, tiled=True
        ).astype(jnp.float32),
        lax.psum_scatter(
            grad_output.astype(jnp.bfloat16), "expert", scatter_dimension=1, tiled=True
        ).astype(jnp.float32),
        lax.psum_scatter(
            grad_ffn_gain.astype(jnp.bfloat16), "expert", scatter_dimension=0, tiled=True
        ).astype(jnp.float32),
        lax.psum_scatter(
            grad_router.astype(jnp.bfloat16), "expert", scatter_dimension=0, tiled=True
        ).astype(jnp.float32),
        lax.psum_scatter(
            grad_shared_gate.astype(jnp.bfloat16), "expert", scatter_dimension=0, tiled=True
        ).astype(jnp.float32),
        lax.psum_scatter(
            grad_shared_up.astype(jnp.bfloat16), "expert", scatter_dimension=0, tiled=True
        ).astype(jnp.float32),
        lax.psum_scatter(
            grad_shared_down.astype(jnp.bfloat16), "expert", scatter_dimension=1, tiled=True
        ).astype(jnp.float32),
    )
    return (
        output,
        grad_tokens,
        reduced[0],
        reduced[1],
        reduced[2],
        reduced[3],
        reduced[4],
        reduced[5],
        reduced[6],
        reduced[7],
        reduced[8],
        reduced[9],
        reduced[10],
        grad_expert_gate,
        grad_expert_up,
        grad_expert_down,
    )


def solution(mesh):
    return jax.shard_map(
        shards,
        mesh=mesh,
        in_specs=(
            P("expert", None),
            P("expert", None),
            P(),
            P(None, "tensor"),
            P(),
            P(),
            P(None, "tensor"),
            P("tensor", None),
            P(),
            P(),
            P(None, "tensor"),
            P(None, "tensor"),
            P("tensor", None),
            P("expert", None, "tensor"),
            P("expert", None, "tensor"),
            P("expert", "tensor", None),
            P("expert", None),
        ),
        out_specs=(
            P("expert", None),
            P("expert", None),
            P("expert"),
            P("expert", "tensor"),
            P("expert", None),
            P("expert"),
            P("expert", "tensor"),
            P("tensor", "expert"),
            P("expert"),
            P("expert", None),
            P("expert", "tensor"),
            P("expert", "tensor"),
            P("tensor", "expert"),
            P("expert", None, "tensor"),
            P("expert", None, "tensor"),
            P("expert", "tensor", None),
        ),
        check_vma=False,
    )
```

profile of v0, /device:TPU:0, one launch (start us, length us, event | category | flops | bytes accessed | tf_op | source)
XLA Modules:
  0.0 1338.4 jit_solution(2130836291980188667)
XLA Ops:
  9.0 3.0 fusion.94
  14.7 2.1 copy.170
  17.8 2.7 fusion.92
  27.2 6.2 scatter_custom_fusion
  33.4 40.7 %all-reduce.11.cloned.1.call-done = bf16[256,2048]{1,0:T(8,128)(2,1)} async-done(((bf16[256,2048]{1,0:T(8,128)(2,1)}), bf16[256,2048]{1,0:T(8,128)(2,1)}) %all-reduce.11.cloned.1.call-update) | async-done | bytes 1048592 | tf_op jit(solution)/shard_map/psum | solution.py:141
  76.1 2.0 multiply_convert_fusion.1
  80.2 17.7 %gather_fusion = bf16[2048,2048]{1,0:T(8,128)(2,1)} fusion(bf16[257,2048]{1,0:T(8,128)(2,1)} %concatenate.31, s32[2048]{0:T(1024)S(1)} %get-tuple-element.49), kind=kCustom, calls=%fused_computation | custom fusion | bytes 16785408 | tf_op jit(solution)/shard_map/gather | solution.py:172
  97.9 19.0 %all-to-all-start = ((bf16[32,2,32,2048]{3,2,1,0:T(8,128)(2,1)}), bf16[32,2,32,2048]{3,2,1,0:T(8,128)(2,1)}, u32[]{:S(2)}, u32[]{:S(2)}) async-start(bf16[32,2,32,2048]{3,2,1,0:T(8,128)(2,1)} %bitcast.159), calls=%async_computation | async-start | bytes 16777216 | tf_op jit(solution)/shard_map/all_to_all | solution.py:173
  116.9 9.1 mul.544
  126.0 15.7 %mul.545 = f32[1536,2048]{1,0:T(8,128)} reshape(f32[256,6,2048]{2,1,0:T(8,128)} %mul.544) | data formatting | bytes 25165824 | tf_op jit(solution)/shard_map/mul | solution.py:199
  144.4 8.0 multiply_convert_fusion
  152.3 6.6 concatenate.32
  159.0 20.0 %gather_fusion.2 = bf16[2048,2048]{1,0:T(8,128)(2,1)} fusion(bf16[1537,2048]{1,0:T(8,128)(2,1)} %concatenate.32, s32[2048]{0:T(1024)S(1)} %get-tuple-element.48), kind=kCustom, calls=%fused_computation.2 | custom fusion | bytes 16785408 | tf_op jit(solution)/shard_map/gather | solution.py:204
  178.9 43.4 %all-to-all-done = bf16[32,2,32,2048]{3,2,1,0:T(8,128)(2,1)} async-done(((bf16[32,2,32,2048]{3,2,1,0:T(8,128)(2,1)}), bf16[32,2,32,2048]{3,2,1,0:T(8,128)(2,1)}, u32[]{:S(2)}, u32[]{:S(2)}) %all-to-all-start) | async-done | bytes 8388640 | tf_op jit(solution)/shard_map/all_to_all | solution.py:173
  222.4 5.0 all-to-all-start.2
  227.4 10.5 fusion.5
  237.9 8.5 fusion.7
  246.4 86.8 %all-to-all-done.2 = bf16[32,2,32,2048]{3,2,1,0:T(8,128)(2,1)} async-done(((bf16[32,2,32,2048]{3,2,1,0:T(8,128)(2,1)}), bf16[32,2,32,2048]{3,2,1,0:T(8,128)(2,1)}, u32[]{:S(2)}, u32[]{:S(2)}) %all-to-all-start.2) | async-done | bytes 8388640 | tf_op jit(solution)/shard_map/all_to_all | solution.py:205
  333.2 13.4 fusion.16
  346.6 10.6 fusion.28
  357.2 11.0 fusion
  368.2 8.3 copy.147
  376.5 5.0 all-to-all-start.3
  381.8 3.2 fusion.97
  389.9 2.3 fusion.100
  392.3 95.1 %all-to-all-done.3 = bf16[32,2,32,2048]{3,2,1,0:T(8,128)(2,1)} async-done(((bf16[32,2,32,2048]{3,2,1,0:T(8,128)(2,1)}), bf16[32,2,32,2048]{3,2,1,0:T(8,128)(2,1)}, u32[]{:S(2)}, u32[]{:S(2)}) %all-to-all-start.3) | async-done | bytes 8388640 | tf_op jit(solution)/shard_map/all_to_all | solution.py:228
  487.3 17.4 %gather_fusion.3 = bf16[1536,2048]{1,0:T(8,128)(2,1)} fusion(bf16[2048,2048]{1,0:T(8,128)(2,1)} %bitcast.22, s32[2048]{0:T(1024)S(1)} %pad_clamp_fusion), kind=kCustom, calls=%fused_computation.3 | custom fusion | bytes 12589056 | tf_op jit(solution)/shard_map/gather | solution.py:231
  504.7 11.7 reshape.314
  516.4 9.8 reduce_sum.201
  526.2 5.2 fusion.34
  531.5 4.0 convolution_convert_fusion.2
  535.5 10.1 convert_bitcast_fusion
  545.6 8.3 copy.143
  553.9 5.0 all-to-all-start.1
  558.9 4.0 convolution_convert_fusion.1
  563.3 2.9 convert_element_type.248
  566.2 2.7 convolution_convert_fusion
  569.0 100.3 %all-to-all-done.1 = bf16[32,2,32,2048]{3,2,1,0:T(8,128)(2,1)} async-done(((bf16[32,2,32,2048]{3,2,1,0:T(8,128)(2,1)}), bf16[32,2,32,2048]{3,2,1,0:T(8,128)(2,1)}, u32[]{:S(2)}, u32[]{:S(2)}) %all-to-all-start.1) | async-done | bytes 8388640 | tf_op jit(solution)/shard_map/all_to_all | solution.py:182
  669.3 17.2 %gather_fusion.1 = bf16[1536,2048]{1,0:T(8,128)(2,1)} fusion(bf16[2048,2048]{1,0:T(8,128)(2,1)} %bitcast.15, s32[2048]{0:T(1024)S(1)} %pad_clamp_fusion), kind=kCustom, calls=%fused_computation.1 | custom fusion | bytes 12589056 | tf_op jit(solution)/shard_map/gather | solution.py:185
  686.5 11.7 reshape.313
  698.2 12.5 multiply_reduce_fusion
  711.6 10.5 psum.52
  722.3 4.5 fusion.35
  726.9 3.7 multiply_reduce_fusion.2
  743.1 2.5 convolution_convert_fusion.8
  745.7 2.7 convolution_convert_fusion.9
  748.5 3.9 convolution_convert_fusion.5
  752.5 4.1 convolution_convert_fusion.3
  761.3 8.8 reduce-scatter.21.cloned.1.call-done
  771.7 82.3 %reduce-scatter.23.cloned.1.call-done = bf16[704,64]{0,1:T(8,128)(2,1)} async-done(((bf16[704,2048]{0,1:T(8,128)(2,1)}), bf16[704,64]{0,1:T(8,128)(2,1)}) %reduce-scatter.23.cloned.1.call-update) | async-done | bytes 90128 | tf_op jit(solution)/shard_map/reduce_scatter | solution.py:333
  855.5 9.6 convolution_bitcast_fusion
  865.2 9.1 convolution_bitcast_fusion.1
  875.2 18.0 %psum.55 = bf16[256,64]{0,1:T(8,128)(2,1)S(1)} all-reduce(bf16[256,64]{0,1:T(8,128)(2,1)S(1)} %slice_reduce_fusion), channel_id=1, replica_groups=mesh['expert'=32,'tensor'=4] {'tensor'}, use_global_device_ids=true, to_apply=%region_27.28 | all-reduce | flops 16384 | bytes 65536 | tf_op jit(solution)/shard_map/psum | solution.py:289
  893.4 26.7 %all-reduce.15.cloned.1.call-done = (bf16[256,2048]{1,0:T(8,128)(2,1)}, bf16[256,2048]{1,0:T(8,128)(2,1)}, bf16[256,512]{0,1:T(8,128)(2,1)}) async-done(((bf16[256,2048]{1,0:T(8,128)(2,1)}, bf16[256,2048]{1,0:T(8,128)(2,1)}, bf16[256,512]{0,1:T(8,128)(2,1)}), (bf16[256,2048]{1,0:T(8,128)(2,1)}, bf16[256,2048]{1,0:T(8,128)(2,1)}, bf16[256,512]{0,1:T(8,128)(2,1)})) %all-reduce.15.cloned.1.call-update) | async-done | bytes 2359312 | tf_op jit(solution)/shard_map/psum | solution.py:187
  922.8 3.9 convolution_convert_fusion.4
  926.7 9.6 fusion.9
  936.3 64.6 %reduce-scatter.17.cloned.1.call-done = bf16[64,64]{1,0:T(8,128)(2,1)} async-done(((bf16[2048,64]{1,0:T(8,128)(2,1)}), bf16[64,64]{1,0:T(8,128)(2,1)}) %reduce-scatter.17.cloned.1.call-update) | async-done | bytes 8208 | tf_op jit(solution)/shard_map/reduce_scatter | solution.py:324
  1002.2 80.1 %reduce-scatter.13.cloned.1.call-done = bf16[16,1024]{1,0:T(8,128)(2,1)} async-done(((bf16[512,1024]{1,0:T(8,128)(2,1)}), bf16[16,1024]{1,0:T(8,128)(2,1)}) %reduce-scatter.13.cloned.1.call-update) | async-done | bytes 32784 | tf_op jit(solution)/shard_map/reduce_scatter | solution.py:315
  1083.6 5.0 fusion.42
  1088.7 65.4 %all-reduce.5 = (bf16[2048]{0:T(1024)(128)(2,1)S(1)}, bf16[512]{0:T(512)(128)(2,1)S(1)}, bf16[2048]{0:T(1024)(128)(2,1)S(1)}) all-reduce(bf16[2048]{0:T(1024)(128)(2,1)S(1)} %get-tuple-element.20, bf16[512]{0:T(512)(128)(2,1)S(1)} %get-tuple-element.22, ...), channel_id=2, replica_groups=mesh['expert'=32,'tensor'=4] {'expert'}, use_global_device_ids=true, to_apply=%region_30.31.clone | all-reduce | flops 4608 | bytes 18432
  1155.3 5.6 fusion.41
  1160.9 3.1 reduce-scatter.15.cloned.1.call-done
  1165.6 81.7 %reduce-scatter.9.cloned.1.call-done = bf16[64,768]{1,0:T(8,128)(2,1)} async-done(((bf16[2048,768]{1,0:T(8,128)(2,1)}), bf16[64,768]{1,0:T(8,128)(2,1)}) %reduce-scatter.9.cloned.1.call-update) | async-done | bytes 98320 | tf_op jit(solution)/shard_map/reduce_scatter | solution.py:306
  1248.9 81.2 %reduce-scatter.11.cloned.1.call-done = bf16[64,576]{1,0:T(8,128)(2,1)} async-done(((bf16[2048,576]{1,0:T(8,128)(2,1)}), bf16[64,576]{1,0:T(8,128)(2,1)}) %reduce-scatter.11.cloned.1.call-update) | async-done | bytes 73744 | tf_op jit(solution)/shard_map/reduce_scatter | solution.py:309
  (253 shorter events, 56.4 us)
Async XLA Ops:
  7.2 10.6 copy-start
  7.2 66.9 %all-reduce.11.cloned.1.call-start = ((), (), s32[]{:S(2)}) async-start(), calls=%async_computation.12 | async-start | bytes 2097152 | tf_op jit(solution)/shard_map/psum | solution.py:141
  7.3 5.0 copy-start.68
  8.9 4.4 copy-start.27
  8.9 4.4 copy-start.52
  9.0 8.8 copy-start.64
  12.0 5.8 copy-start.54
  12.5 8.1 copy-start.31
  12.5 8.1 copy-start.33
  17.8 2.9 copy-start.35
  20.5 2.2 copy-start.22
  21.8 2.2 copy-start.12
  23.3 2.4 copy-start.40
  25.7 50.4 %copy-start.50 = (f32[2048]{0:T(1024)S(1)}, f32[2048]{0:T(1024)}, u32[]{:S(2)}) copy-start(f32[2048]{0:T(1024)} %param.25) | copy-start | bytes 24580
  76.1 21.8 %copy-start.66 = (f32[256]{0:T(256)}, f32[256]{0:T(256)S(1)}, u32[]{:S(2)}) copy-start(f32[256]{0:T(256)S(1)} %add_rsqrt_fusion) | copy-start | bytes 3076
  97.9 124.5 %all-to-all-start = ((bf16[32,2,32,2048]{3,2,1,0:T(8,128)(2,1)}), bf16[32,2,32,2048]{3,2,1,0:T(8,128)(2,1)}, u32[]{:S(2)}, u32[]{:S(2)}) async-start(bf16[32,2,32,2048]{3,2,1,0:T(8,128)(2,1)} %bitcast.159), calls=%async_computation | async-start | bytes 16777216 | tf_op jit(solution)/shard_map/all_to_all | solution.py:173
  126.0 15.7 %copy-start.39 = (bf16[2048,64]{0,1:T(8,128)(2,1)S(1)}, bf16[2048,64]{0,1:T(8,128)(2,1)}, u32[]{:S(2)}) copy-start(bf16[2048,64]{0,1:T(8,128)(2,1)} %param.26) | copy-start | bytes 786436
  144.1 8.3 copy-start.62
  144.2 8.1 copy-start.26
  222.4 110.9 %all-to-all-start.2 = ((bf16[32,2,32,2048]{3,2,1,0:T(8,128)(2,1)}), bf16[32,2,32,2048]{3,2,1,0:T(8,128)(2,1)}, u32[]{:S(2)}, u32[]{:S(2)}) async-start(bf16[32,2,32,2048]{3,2,1,0:T(8,128)(2,1)} %bitcast.160), calls=%async_computation.2 | async-start | bytes 16777216 | tf_op jit(solution)/shard_map/all_to_all | solution.py:205
  227.4 10.5 copy-start.19
  346.6 10.6 copy-start.14
  346.6 10.6 copy-start.16
  376.5 110.9 %all-to-all-start.3 = ((bf16[32,2,32,2048]{3,2,1,0:T(8,128)(2,1)}), bf16[32,2,32,2048]{3,2,1,0:T(8,128)(2,1)}, u32[]{:S(2)}, u32[]{:S(2)}) async-start(bf16[32,2,32,2048]{3,2,1,0:T(8,128)(2,1)} %copy.147), calls=%async_computation.3 | async-start | bytes 16777216 | tf_op jit(solution)/shard_map/all_to_all | solution.py:228
  381.5 345.4 %all-reduce.13.cloned.1.call-start = ((), (), s32[]{:S(2)}) async-start(), calls=%async_computation.13 | async-start | bytes 2097152 | tf_op jit(solution)/shard_map/psum | solution.py:234
  381.8 3.3 copy-start.2
  381.8 3.3 copy-start.17
  385.1 2.1 copy-start.18
  387.3 2.7 copy-start.20
  531.4 228.2 %reduce-scatter.19.cloned.1.call-start = ((), (), s32[]{:S(2)}) async-start(), calls=%async_computation.19 | async-start | bytes 3244032 | tf_op jit(solution)/shard_map/reduce_scatter | solution.py:327
  553.9 115.4 %all-to-all-start.1 = ((bf16[32,2,32,2048]{3,2,1,0:T(8,128)(2,1)}), bf16[32,2,32,2048]{3,2,1,0:T(8,128)(2,1)}, u32[]{:S(2)}, u32[]{:S(2)}) async-start(bf16[32,2,32,2048]{3,2,1,0:T(8,128)(2,1)} %copy.143), calls=%async_computation.1 | async-start | bytes 16777216 | tf_op jit(solution)/shard_map/all_to_all | solution.py:182
  558.9 211.2 %reduce-scatter.21.cloned.1.call-start = ((), (), s32[]{:S(2)}) async-start(), calls=%async_computation.20 | async-start | bytes 3244032 | tf_op jit(solution)/shard_map/reduce_scatter | solution.py:330
  563.0 3.2 copy-start.59
  563.0 3.2 copy-start.61
  563.0 290.9 %reduce-scatter.23.cloned.1.call-start = ((), (), s32[]{:S(2)}) async-start(), calls=%async_computation.21 | async-start | bytes 3244032 | tf_op jit(solution)/shard_map/reduce_scatter | solution.py:333
  563.3 2.9 copy-start.6
  569.0 351.1 %all-reduce.15.cloned.1.call-start = ((), (), s32[]{:S(2)}) async-start(), calls=%async_computation.22 | async-start | bytes 4718592 | tf_op jit(solution)/shard_map/psum | solution.py:187
  698.2 24.0 %copy-start.43 = (f32[256,6]{0,1:T(8,128)S(1)}, f32[256,6]{0,1:T(8,128)}, u32[]{:S(2)}) copy-start(f32[256,6]{0,1:T(8,128)} %copy-done.42) | copy-start | bytes 18436
  698.2 24.0 %copy-start.63 = (f32[256]{0:T(256)S(1)}, f32[256]{0:T(256)}, u32[]{:S(2)}) copy-start(f32[256]{0:T(256)} %copy-done.62) | copy-start | bytes 3076
  722.3 4.6 copy-start.41
  722.3 4.6 copy-start.51
  722.3 4.6 copy-start.67
  726.9 3.7 copy-start.3
  726.9 3.7 copy-start.7
  726.9 3.7 copy-start.8
  730.7 2.2 copy-start.13
  734.3 3.2 copy-start.47
  735.4 1.9 copy-start.10
  735.4 2.1 copy-start.38
  735.4 2.1 copy-start.49
  738.6 2.4 copy-start.23
  743.0 2.7 copy-start.53
  743.0 2.7 copy-start.57
  743.0 257.8 %reduce-scatter.17.cloned.1.call-start = ((), (), s32[]{:S(2)}) async-start(), calls=%async_computation.18 | async-start | bytes 540672 | tf_op jit(solution)/shard_map/reduce_scatter | solution.py:324
  745.6 336.6 %reduce-scatter.13.cloned.1.call-start = ((), (), s32[]{:S(2)}) async-start(), calls=%async_computation.16 | async-start | bytes 1081344 | tf_op jit(solution)/shard_map/reduce_scatter | solution.py:315
  748.4 4.1 copy-start.24
  748.4 4.1 copy-start.55
  748.4 415.7 %reduce-scatter.15.cloned.1.call-start = ((), (), s32[]{:S(2)}) async-start(), calls=%async_computation.17 | async-start | bytes 2162688 | tf_op jit(solution)/shard_map/reduce_scatter | solution.py:318
  752.4 494.9 %reduce-scatter.9.cloned.1.call-start = ((), (), s32[]{:S(2)}) async-start(), calls=%async_computation.14 | async-start | bytes 3244032 | tf_op jit(solution)/shard_map/reduce_scatter | solution.py:306
  756.6 573.5 %reduce-scatter.11.cloned.1.call-start = ((), (), s32[]{:S(2)}) async-start(), calls=%async_computation.15 | async-start | bytes 2703360 | tf_op jit(solution)/shard_map/reduce_scatter | solution.py:309
  855.5 9.6 copy-start.15
  865.2 28.1 %copy-start.69 = (f32[32]{0:T(128)S(1)}, f32[32]{0:T(128)}, u32[]{:S(2)}) copy-start(f32[32]{0:T(128)} %copy-done.68) | copy-start | bytes 388
  865.2 57.6 %copy-start.65 = (f32[256]{0:T(256)S(1)}, f32[256]{0:T(256)}, u32[]{:S(2)}) copy-start(f32[256]{0:T(256)} %copy-done.64) | copy-start | bytes 3076
  1083.6 5.0 copy-start.70
  (22 other events, 20.2 us)
Sparse Core Ops, SparseCore 0:
  25.9 48.1 all-reduce.10
  531.6 42.2 all-reduce.12
  578.0 107.6 reduce-scatter.18
  690.3 79.7 reduce-scatter.20
  774.1 79.7 reduce-scatter.22
  857.1 62.9 all-reduce.14
  923.9 76.8 reduce-scatter.16
  1005.3 76.8 reduce-scatter.12
  1085.8 78.2 reduce-scatter.14
  1167.5 79.7 reduce-scatter.8
  1251.3 78.7 reduce-scatter.10
where the time goes:
time: 1340 us
  waiting for transfers between devices  795 us (59%)
  local copies, waits for them, and re-layouts  168 us (13%)
  matrix products  166 us (12%)
  blocking collectives  93.9 us (7%)
  other arithmetic  64.7 us (5%)
  starting transfers between devices  35.1 us (3%)
  between operations  16.5 us (1%)
    all_to_all x1, waiting for transfers between devices, shards(): lax.all_to_all(produced, 'expert', split_axis=0, concat_axis=0, tiled=True)  100 us
    all_to_all x1, waiting for transfers between devices, shards(): lax.all_to_all(row_grad, 'expert', split_axis=0, concat_axis=0, tiled=True)  95.1 us
    all_to_all x1, waiting for transfers between devices, shards(): lax.all_to_all(outgoing_grad, 'expert', split_axis=0, concat_axis=0, tile...  86.8 us
    reduce_scatter x1, waiting for transfers between devices, shards(): lax.psum_scatter(grad_shared_down.astype(jnp.bfloat16), 'expert', scatter...  82.3 us
    reduce_scatter x1, waiting for transfers between devices, shards(): lax.psum_scatter(grad_query.astype(jnp.bfloat16), 'expert', scatter_dimen...  81.7 us
    reduce_scatter x1, waiting for transfers between devices, shards(): lax.psum_scatter(grad_latent.astype(jnp.bfloat16), 'expert', scatter_dime...  81.2 us
    reduce_scatter x1, waiting for transfers between devices, shards(): lax.psum_scatter(grad_keyvalue.astype(jnp.bfloat16), 'expert', scatter_di...  80.1 us
    dot_general x24, matrix products, matmul(): return jnp.dot(left_side, right_side, preferred_element_type=jnp.float32)  69.7 us
  transfers between devices with their start and end apart: 15, of which 13 were waited for; matrix products, arithmetic and copies ran while one was open for 20% of the time, Pallas kernels for 0%

commit v1 on v0

v1 whole, which is shorter than its diff:
```python
import functools
import math

import jax
import jax.numpy as jnp
import numpy as np
from jax import lax
from jax.experimental import pallas as pl
from jax.experimental.pallas import tpu as pltpu
from jax.sharding import PartitionSpec as P

NOPE = 128
ROPE = 64
VDIM = 128
KV_RANK = 512


EPS = 1e-06
THETA = 50000.0
ROUTE_SCALE = 2.446
MASKED = -1e30
LANES = 128


def rms_scale(values):
    return lax.rsqrt(jnp.mean(values * values, axis=-1, keepdims=True) + EPS)


def unrotary(grads_in, cosine_table, sine_table):
    half_width = grads_in.shape[-1] // 2
    former = grads_in[..., :half_width]
    latter = grads_in[..., half_width:]
    return jnp.concatenate(
        [former * cosine_table + latter * sine_table, latter * cosine_table - former * sine_table],
        axis=-1,
    )


def silu_back(grad_act, gate_pre, up_pre):
    sigma_gate = jax.nn.sigmoid(gate_pre)
    grad_up = grad_act * gate_pre * sigma_gate
    grad_gate = grad_act * up_pre * sigma_gate * (1.0 + gate_pre * (1.0 - sigma_gate))
    return (grad_gate.astype(jnp.bfloat16), grad_up.astype(jnp.bfloat16))


def matmul(left_side, right_side):
    return jnp.dot(left_side, right_side, preferred_element_type=jnp.float32)


def matmul_tn(left_side, right_side):
    return lax.dot_general(
        left_side, right_side, (((0,), (0,)), ((), ())), preferred_element_type=jnp.float32
    )


def matmul_nt(left_side, right_side):
    return lax.dot_general(
        left_side, right_side, (((1,), (1,)), ((), ())), preferred_element_type=jnp.float32
    )


def two_parts(values):
    high = lax.reduce_precision(values, 8, 7)
    return (high.astype(jnp.bfloat16), (values - high).astype(jnp.bfloat16))


def after(value, *others):
    return lax.optimization_barrier((value,) + others)[0]


def shift_ranks(values, step, count):
    return lax.ppermute(values, "tensor", [(i, (i + step) % count) for i in range(count)])


def column_block(values, index, width):
    return lax.dynamic_slice_in_dim(values, index * width, width, axis=1)


def gather_columns(block, rank, count, width):
    pieces = [block] + [shift_ranks(block, step, count) for step in range(1, count)]
    ordered = [
        lax.select_n(lax.rem(rank - place + count, count), *[p[:, :width] for p in pieces])
        for place in range(count)
    ]
    return (jnp.concatenate(ordered, axis=1), [p[:, width:] for p in pieces])


def expert_rows_kernel(sideways, first_ref, x_ref, gate_ref, g_ref, wgu_ref, wgut_ref, wd_ref, wdt_ref,
                       *rest):
    produced_ref, rowgrad_ref, dgu_ref, actw_ref = rest[-4:]
    quarters, step, cap, part = g_ref.shape
    rows = step * cap
    width, model = wd_ref.shape
    half = LANES // 2
    expert = first_ref[0]
    column = lax.broadcasted_iota(jnp.int32, (rows, LANES), 1)
    chosen = (column == expert) | (column == expert + half)
    gates = gate_ref[...].reshape(rows, LANES).astype(jnp.float32)
    weight = jnp.sum(jnp.where(chosen, gates, 0.0), axis=1, keepdims=True)

    def by_quarters(values_ref, matrix_ref):
        total = matmul(values_ref[0].reshape(rows, part), matrix_ref[:part, :])
        for place in range(1, quarters):
            total += matmul(
                values_ref[place].reshape(rows, part),
                matrix_ref[place * part:(place + 1) * part, :],
            )
        return total

    pre = matmul(x_ref[...].reshape(rows, model), wgu_ref[...])
    grad_act = by_quarters(g_ref, wdt_ref)
    gate_pre = pre[:, :width]
    up_pre = pre[:, width:]
    sigma = 1.0 / (1.0 + jnp.exp(-gate_pre))
    silu = gate_pre * sigma
    act = silu * up_pre
    act_weighted = (act * weight).astype(jnp.bfloat16)
    actw_ref[...] = act_weighted
    for place in range(quarters):
        out = matmul(act_weighted, wd_ref[:, place * part:(place + 1) * part])
        produced_ref[place] = out.astype(jnp.bfloat16).reshape(step, cap, part)
    dot = jnp.sum(grad_act * act, axis=1, keepdims=True)
    grad_act = grad_act * weight
    grad_up = grad_act * silu
    grad_gate = grad_act * up_pre * (sigma + silu * (1.0 - sigma))
    row_dot = jnp.sum(grad_gate * gate_pre + grad_up * up_pre, axis=1, keepdims=True)
    row_dot_high = row_dot.astype(jnp.bfloat16).astype(jnp.float32)
    pre_grad = jnp.concatenate([grad_gate, grad_up], axis=1).astype(jnp.bfloat16)
    dgu_ref[...] = pre_grad
    row_grad = matmul(pre_grad, wgut_ref[...]).astype(jnp.bfloat16)
    sums = jnp.where(column == expert, dot, 0.0)
    sums = jnp.where(column == half, row_dot_high, sums)
    sums = jnp.where(column == half + 1, row_dot - row_dot_high, sums)
    sums = sums.astype(jnp.bfloat16).reshape(step, cap, LANES)
    if sideways:
        for place in range(quarters):
            rowgrad_ref[place, :, :, :part] = (
                row_grad[:, place * part:(place + 1) * part].reshape(step, cap, part)
            )
            rowgrad_ref[place, :, :, part:] = sums
    else:
        rowgrad_ref[:, :, :model] = row_grad.reshape(step, cap, model)
        rowgrad_ref[:, :, model:] = sums


def expert_rows(number, first, x, g, weights, sideways, produced=None):
    quarters, sources, experts, cap, part = g.shape
    wgu, wgut, wd, wdt = weights
    width, model = wd.shape[1:]
    step = 16
    rows = step * cap
    total = sources * cap

    def flat_block(columns):
        return pl.BlockSpec((rows, columns), lambda b, f: (b, 0))

    def whole(*shape):
        return pl.BlockSpec((None,) + shape, lambda b, f: (number, 0, 0))

    def kind(*shape):
        return jax.ShapeDtypeStruct(shape, jnp.bfloat16)

    def part_block(columns):
        return pl.BlockSpec((quarters, step, cap, columns), lambda b, f: (0, b, 0, 0))

    def row_block(columns):
        return pl.BlockSpec((step, cap, columns), lambda b, f: (b, 0, 0))

    expert_part = pl.BlockSpec(
        (quarters, step, None, cap, part), lambda b, f: (0, b, number, 0, 0)
    )
    last = model // LANES
    in_specs = [
        pl.BlockSpec((step, None, cap, model), lambda b, f: (b, number, 0, 0)),
        pl.BlockSpec((step, None, cap, LANES), lambda b, f: (b, number, 0, last)), expert_part,
        whole(model, 2 * width), whole(2 * width, model), whole(width, model), whole(model, width),
    ]
    inputs = ()
    aliases = {}
    if produced is not None:
        inputs = (produced,)
        in_specs.append(pl.BlockSpec(memory_space=pl.ANY))
        aliases = {len(in_specs): 0}
    return pl.pallas_call(
        functools.partial(expert_rows_kernel, sideways),
        grid_spec=pltpu.PrefetchScalarGridSpec(
            num_scalar_prefetch=1,
            grid=(sources // step,),
            in_specs=in_specs,
            out_specs=[
                expert_part, part_block(part + LANES) if sideways else row_block(model + LANES),
                flat_block(2 * width), flat_block(width),
            ],
        ),
        out_shape=[
            kind(*g.shape),
            kind(quarters, sources, cap, part + LANES) if sideways
            else kind(sources, cap, model + LANES),
            kind(total, 2 * width), kind(total, width),
        ],
        compiler_params=pltpu.CompilerParams(vmem_limit_bytes=60 * 1024 * 1024),
        cost_estimate=pl.CostEstimate(
            flops=2 * total * model * width * 6, bytes_accessed=30_000_000,
            transcendentals=total * width,
        ),
        input_output_aliases=aliases,
        name=f"expert_rows_{number}",
    )(first + number, x, x, g, wgu, wgut, wd, wdt, *inputs)


def expert_weights_kernel(x_ref, g_ref, dgu_ref, actw_ref, *rest):
    gate_ref, up_ref, down_ref = rest[-3:]
    rows, width = actw_ref.shape
    hidden = gate_ref.shape[0]
    grad = matmul_tn(dgu_ref[...], x_ref[...].reshape(rows, x_ref.shape[-1]))
    gate_ref[...] = grad[:hidden, :]
    up_ref[...] = grad[width:width + hidden, :]
    g_rows = g_ref[...].reshape(rows, g_ref.shape[-1])
    down_ref[...] = matmul_tn(actw_ref[...], g_rows)[:hidden, :]


def expert_weights(number, x, g, dgu, actw, hidden, before=()):
    quarters, sources, experts, cap, quarter = g.shape
    model = quarters * quarter
    total, width = actw.shape
    steps = 8
    part = model // steps
    per = steps // quarters
    x_block = pl.BlockSpec((sources, None, cap, part), lambda b: (0, number, 0, b))
    in_specs = [
        x_block,
        pl.BlockSpec((None, sources, None, cap, part),
                     lambda b: (b // per, 0, number, 0, b % per)),
        pl.BlockSpec((total, 2 * width), lambda b: (0, 0)),
        pl.BlockSpec((total, width), lambda b: (0, 0)),
    ] + [pl.BlockSpec(memory_space=pl.ANY)] * len(before)
    return pl.pallas_call(
        expert_weights_kernel,
        grid=(steps,),
        in_specs=in_specs,
        out_specs=[pl.BlockSpec((None, hidden, part), lambda b: (number, 0, b))] * 3,
        out_shape=[jax.ShapeDtypeStruct((experts, hidden, model), jnp.float32)] * 3,
        compiler_params=pltpu.CompilerParams(vmem_limit_bytes=56 * 1024 * 1024),
        cost_estimate=pl.CostEstimate(
            flops=2 * total * model * width * 3, bytes_accessed=22_000_000, transcendentals=0
        ),
        input_output_aliases={4 + place: place for place in range(len(before))},
        name=f"expert_weights_{number}",
    )(x, g, dgu, actw, *before)


def shared_weights_kernel(n_ref, c_ref, gate_ref, up_ref, act_ref, out_ref):
    chunk = out_ref.shape[1] // 3
    for place, (rows, grads) in enumerate(
        ((n_ref, gate_ref), (n_ref, up_ref), (c_ref, act_ref))
    ):
        grad = matmul_tn(rows[...], grads[...]).astype(jnp.bfloat16)
        for group in range(out_ref.shape[0]):
            out_ref[group, place * chunk:(place + 1) * chunk, :] = (
                grad[group * chunk:(group + 1) * chunk, :]
            )


def shared_weights(normed, cotangent, gate_grad, up_grad, act, groups):
    tokens, model = normed.shape
    width = gate_grad.shape[1]
    block = 256
    chunk = model // groups
    per = block // chunk
    rows = pl.BlockSpec((tokens, block), lambda i: (0, i))
    grads = pl.BlockSpec((tokens, width), lambda i: (0, 0))
    return pl.pallas_call(
        shared_weights_kernel,
        grid=(model // block,),
        in_specs=[rows, rows, grads, grads, grads],
        out_specs=pl.BlockSpec((per, 3 * chunk, width), lambda i: (i, 0, 0)),
        out_shape=jax.ShapeDtypeStruct((groups, 3 * chunk, width), jnp.bfloat16),
        compiler_params=pltpu.CompilerParams(vmem_limit_bytes=48 * 1024 * 1024),
        cost_estimate=pl.CostEstimate(
            flops=6 * tokens * model * width, bytes_accessed=14_000_000, transcendentals=0
        ),
        name="shared_weights",
    )(normed, cotangent, gate_grad, up_grad, act)


def combine_kernel(rank_ref, pick_ref, back_ref, sums_ref, shared_ref, dots_ref,
                   own_ref, extra_ref, *sends):
    step = pl.program_id(0)
    count = pl.num_programs(0)
    place = lax.rem(step - rank_ref[0] + count, count)
    part = own_ref.shape[1]
    value = matmul(pick_ref[...], back_ref[...]) + shared_ref[...]

    @pl.when(place == 0)
    def _():
        own_ref[...] = value

    for number, send in enumerate(sends):
        @pl.when(place == number + 1)
        def _():
            send[:, :part] = value.astype(jnp.bfloat16)

    @pl.when(step == count - 1)
    def _():
        mark = LANES // 2
        sums = matmul(pick_ref[...], sums_ref[...])
        column = lax.broadcasted_iota(jnp.int32, sums.shape, 1)
        mean = dots_ref[...] + jnp.sum(
            jnp.where((column == mark) | (column == mark + 1), sums, 0.0), axis=1, keepdims=True
        )
        mean_high = mean.astype(jnp.bfloat16).astype(jnp.float32)
        extra = jnp.where(column < mark, sums, 0.0)
        extra = jnp.where(column == mark, mean_high, extra)
        extra = jnp.where(column == mark + 1, mean - mean_high, extra).astype(jnp.bfloat16)
        extra_ref[...] = extra
        for send in sends:
            send[:, part:] = extra


def combine_rows(rank, pick, back, shared, dots, count):
    tokens, slots = pick.shape
    model = shared.shape[1]
    part = model // count
    sent = jax.ShapeDtypeStruct((tokens, part + LANES), jnp.bfloat16)
    sent_block = pl.BlockSpec((tokens, part + LANES), lambda i, r: (0, 0))
    return pl.pallas_call(
        combine_kernel,
        grid_spec=pltpu.PrefetchScalarGridSpec(
            num_scalar_prefetch=1,
            grid=(count,),
            in_specs=[
                pl.BlockSpec((tokens, slots), lambda i, r: (0, 0)),
                pl.BlockSpec((slots, part), lambda i, r: (0, i)),
                pl.BlockSpec((slots, LANES), lambda i, r: (0, model // LANES)),
                pl.BlockSpec((tokens, part), lambda i, r: (0, i)),
                pl.BlockSpec((tokens, 1), lambda i, r: (0, 0)),
            ],
            out_specs=[
                pl.BlockSpec((tokens, part), lambda i, r: (0, 0)),
                pl.BlockSpec((tokens, LANES), lambda i, r: (0, 0)),
            ] + [sent_block] * (count - 1),
        ),
        out_shape=[
            jax.ShapeDtypeStruct((tokens, part), jnp.float32),
            jax.ShapeDtypeStruct((tokens, LANES), jnp.bfloat16),
        ] + [sent] * (count - 1),
        compiler_params=pltpu.CompilerParams(vmem_limit_bytes=48 * 1024 * 1024),
        cost_estimate=pl.CostEstimate(
            flops=2 * tokens * slots * model, bytes_accessed=9_000_000, transcendentals=0
        ),
        name="combine_rows",
    )(rank.reshape(1), pick, back, back, shared, dots)


def attention_forward_kernel(rank_ref, token_ref, gain_ref, latent_gain_ref, cosine_ref, ahead_ref,
                             behind_ref, key_cosine_ref, key_sine_ref, w_latent_ref, w_query_ref,
                             w_keyvalue_ref, w_output_ref,
                             normed_ref, scale_ref, query_ref, query_low_ref, latent_ref,
                             latent_normed_ref, keyvalue_ref, key_rope_ref, weights_ref, mixed_ref,
                             own_ref, *rest):
    *sends, latent_buf, query_buf, keyvalue_buf, output_buf, sems = rest
    copies = [
        pltpu.make_async_copy(source, buffer, sems.at[number])
        for number, (source, buffer) in enumerate((
            (w_latent_ref, latent_buf), (w_query_ref, query_buf), (w_keyvalue_ref, keyvalue_buf),
            (w_output_ref, output_buf),
        ))
    ]
    for copy in copies:
        copy.start()
    tokens = token_ref[...].astype(jnp.float32)
    scale = lax.rsqrt(jnp.mean(tokens * tokens, axis=1, keepdims=True) + EPS)
    scale_ref[...] = scale
    normed = (tokens * scale * gain_ref[...]).astype(jnp.bfloat16)
    normed_ref[...] = normed
    copies[0].wait()
    latent = matmul_nt(normed, latent_buf[...])
    latent_ref[...] = latent
    compressed = latent[:, :KV_RANK]
    latent_scale = lax.rsqrt(jnp.mean(compressed * compressed, axis=1, keepdims=True) + EPS)
    latent_normed = (compressed * latent_scale * latent_gain_ref[...]).astype(jnp.bfloat16)
    latent_normed_ref[...] = latent_normed
    half = ROPE // 2
    former = latent[:, KV_RANK:KV_RANK + half]
    latter = latent[:, KV_RANK + half:]
    key_cosine, key_sine = key_cosine_ref[...], key_sine_ref[...]
    key_rope = jnp.concatenate(
        [former * key_cosine - latter * key_sine, latter * key_cosine + former * key_sine], axis=1
    ).astype(jnp.bfloat16)
    key_rope_ref[...] = key_rope
    copies[1].wait()
    query = matmul(normed, query_buf[...])
    query_ref[...] = query
    wide = query.shape[1]
    query_low_ref[...] = (
        query * cosine_ref[...] + pltpu.roll(query, wide - half, 1) * ahead_ref[...]
        + pltpu.roll(query, half, 1) * behind_ref[...]
    ).astype(jnp.bfloat16)
    copies[2].wait()
    keyvalue_ref[...] = matmul(latent_normed, keyvalue_buf[...]).astype(jnp.bfloat16)
    rows = tokens.shape[0]
    causal = (
        lax.broadcasted_iota(jnp.int32, (rows, rows), 0)
        >= lax.broadcasted_iota(jnp.int32, (rows, rows), 1)
    )
    qk_width = NOPE + ROPE
    for head in range(wide // qk_width):
        low = head * (NOPE + VDIM)
        query_head = query_low_ref[:, head * qk_width:(head + 1) * qk_width]
        key_head = jnp.concatenate([keyvalue_ref[:, low:low + NOPE], key_rope], axis=1)
        scores = matmul_nt(query_head, key_head) * (qk_width ** -0.5)
        scores = jnp.where(causal, scores, MASKED)
        terms = jnp.exp(scores - jnp.max(scores, axis=1, keepdims=True))
        weights = terms / jnp.sum(terms, axis=1, keepdims=True)
        weights_ref[head] = weights
        mixed_ref[:, head * VDIM:(head + 1) * VDIM] = matmul(
            weights.astype(jnp.bfloat16), keyvalue_ref[:, low + NOPE:low + NOPE + VDIM]
        ).astype(jnp.bfloat16)
    copies[3].wait()
    part = own_ref.shape[1]
    count = len(sends) + 1
    for number in range(count):
        value = matmul(mixed_ref[...], output_buf[:, number * part:(number + 1) * part])
        place = lax.rem(number - rank_ref[0] + count, count)

        @pl.when(place == 0)
        def _():
            own_ref[...] = value

        for index, send in enumerate(sends):
            @pl.when(place == index + 1)
            def _():
                send[...] = value.astype(jnp.bfloat16)


def rotary_constants(rows, heads):
    half = ROPE // 2
    frequency = np.float32(THETA) ** (np.arange(half, dtype=np.float32) * np.float32(-2.0 / ROPE))
    angles = np.arange(rows, dtype=np.float32)[:, None] * frequency[None, :]
    cosine, sine = np.cos(angles), np.sin(angles)
    blank = np.zeros((rows, NOPE), np.float32)
    zero = np.zeros((rows, half), np.float32)

    def tiled(*pieces):
        return np.tile(np.concatenate(pieces, axis=1), (1, heads)).astype(np.float32)

    return (
        tiled(blank + 1.0, cosine, cosine), tiled(blank, -sine, zero), tiled(blank, zero, sine),
        cosine, sine,
    )


def full_specs(arrays):
    return [pl.BlockSpec(a.shape, lambda i, r, n=len(a.shape): (0,) * n) for a in arrays]


def attention_forward(rank, tokens, gain, latent_gain, tables, w_latent, w_query, w_keyvalue, w_output,
                      count):
    rows, model = tokens.shape
    part = model // count
    latent_width = w_latent.shape[1]
    query_width = w_query.shape[1]
    heads = query_width // (NOPE + ROPE)
    bf16, f32 = jnp.bfloat16, jnp.float32
    out_shape = [
        jax.ShapeDtypeStruct(shape, kind)
        for shape, kind in (
            ((rows, model), bf16), ((rows, 1), f32), ((rows, query_width), f32),
            ((rows, query_width), bf16), ((rows, latent_width), f32), ((rows, KV_RANK), bf16),
            ((rows, w_keyvalue.shape[1]), bf16), ((rows, ROPE), bf16), ((heads, rows, rows), f32),
            ((rows, heads * VDIM), bf16), ((rows, part), f32),
        ) + (((rows, part), bf16),) * (count - 1)
    ]
    inputs = [tokens, gain.reshape(1, -1), latent_gain.reshape(1, -1), *tables]
    streamed = [w_latent.T, w_query, w_keyvalue, w_output]
    return pl.pallas_call(
        attention_forward_kernel,
        grid_spec=pltpu.PrefetchScalarGridSpec(
            num_scalar_prefetch=1,
            grid=(1,),
            in_specs=full_specs(inputs) + [pl.BlockSpec(memory_space=pl.ANY)] * len(streamed),
            out_specs=full_specs(out_shape),
            scratch_shapes=[pltpu.VMEM(a.shape, a.dtype) for a in streamed]
            + [pltpu.SemaphoreType.DMA((len(streamed),))],
        ),
        out_shape=out_shape,
        compiler_params=pltpu.CompilerParams(vmem_limit_bytes=48 * 1024 * 1024),
        cost_estimate=pl.CostEstimate(
            flops=5_000_000_000, bytes_accessed=16_000_000, transcendentals=300_000
        ),
        name="attention_forward",
    )(rank.reshape(1), *inputs, *streamed)


def attention_backward_kernel(rank_ref, *refs):
    count = 4
    pieces, refs = refs[:count], refs[count:]
    (weights_ref, keyvalue_ref, key_rope_ref, query_low_ref, query_ref, token_ref, scale_ref, cosine_ref,
     ahead_ref, behind_ref, w_output_ref, w_keyvalue_ref, w_query_ref,
     branch_ref, gain_ref, query_grad_ref, keyvalue_grad_ref, own_ref, latent_ref, *rest) = refs
    *sends, output_buf, keyvalue_buf, query_buf, grad_buf, sems = rest
    copies = [
        pltpu.make_async_copy(source, buffer, sems.at[number])
        for number, (source, buffer) in enumerate((
            (w_output_ref, output_buf), (w_keyvalue_ref, keyvalue_buf), (w_query_ref, query_buf),
        ))
    ]
    for copy in copies:
        copy.start()
    rows, model = branch_ref.shape
    part = own_ref.shape[1]
    for place in range(count):
        columns = slice(place * part, (place + 1) * part)
        turn = lax.rem(rank_ref[0] - place + count, count)
        for number, piece in enumerate(pieces):
            @pl.when(turn == number)
            def _():
                branch_ref[:, columns] = piece[:rows, :]
                sums = piece[rows:, :].astype(jnp.float32)
                gain_ref[:, columns] = sums[0:1] + sums[1:2]
    copies[0].wait()
    mixed_grad = matmul_nt(branch_ref[...], output_buf[...]).astype(jnp.bfloat16)
    qk_width = NOPE + ROPE
    soft = qk_width ** -0.5
    key_rope = key_rope_ref[...]
    rope_grad = jnp.zeros((rows, ROPE), jnp.float32)
    for head in range(weights_ref.shape[0]):
        low = head * (NOPE + VDIM)
        columns = slice(head * qk_width, (head + 1) * qk_width)
        weights = weights_ref[head]
        out_grad = mixed_grad[:, head * VDIM:(head + 1) * VDIM]
        keyvalue_grad_ref[:, low + NOPE:low + NOPE + VDIM] = matmul_tn(
            weights.astype(jnp.bfloat16), out_grad
        ).astype(jnp.bfloat16)
        prob_grad = matmul_nt(out_grad, keyvalue_ref[:, low + NOPE:low + NOPE + VDIM])
        row_term = jnp.sum(weights * prob_grad, axis=1, keepdims=True)
        score_grad = (weights * (prob_grad - row_term)).astype(jnp.bfloat16)
        key_head = jnp.concatenate([keyvalue_ref[:, low:low + NOPE], key_rope], axis=1)
        grad_buf[:, columns] = matmul(score_grad, key_head) * soft
        key_grad = matmul_tn(score_grad, query_low_ref[:, columns]) * soft
        keyvalue_grad_ref[:, low:low + NOPE] = key_grad[:, :NOPE].astype(jnp.bfloat16)
        rope_grad += key_grad[:, NOPE:]
    grad = grad_buf[...]
    wide = grad.shape[1]
    half = ROPE // 2
    query_grad = (
        grad * cosine_ref[...] - pltpu.roll(grad, wide - half, 1) * ahead_ref[...]
        - pltpu.roll(grad, half, 1) * behind_ref[...]
    ).astype(jnp.bfloat16)
    query_grad_ref[...] = query_grad
    mean = jnp.sum(query_grad.astype(jnp.float32) * query_ref[...], axis=1, keepdims=True)
    mean_high = mean.astype(jnp.bfloat16).astype(jnp.float32)
    copies[1].wait()
    latent_part = matmul_nt(keyvalue_grad_ref[...], keyvalue_buf[...])
    width = latent_part.shape[1]
    column = lax.broadcasted_iota(jnp.int32, (rows, LANES - ROPE), 1)
    sums = jnp.where(column == 0, mean_high, jnp.where(column == 1, mean - mean_high, 0.0))
    latent_ref[:rows, :width] = latent_part.astype(jnp.bfloat16)
    latent_ref[:rows, width:] = jnp.concatenate([rope_grad, sums], axis=1).astype(jnp.bfloat16)
    copies[2].wait()
    gains = []
    scale = scale_ref[...]
    for number in range(count):
        columns = slice(number * part, (number + 1) * part)
        value = matmul_nt(query_grad, query_buf[columns, :])
        unit = token_ref[:, columns].astype(jnp.float32) * scale
        gains.append(jnp.sum(value * unit, axis=0, keepdims=True))
        place = lax.rem(number - rank_ref[0] + count, count)

        @pl.when(place == 0)
        def _():
            own_ref[...] = value

        for index, send in enumerate(sends):
            @pl.when(place == index + 1)
            def _():
                send[:rows, width + LANES:] = value.astype(jnp.bfloat16)
    highs = [gain.astype(jnp.bfloat16).astype(jnp.float32) for gain in gains]
    lows = [gain - high for gain, high in zip(gains, highs)]
    spare = latent_ref.shape[0] - rows
    latent_ref[rows:, :width] = jnp.concatenate(
        highs + lows + [jnp.zeros((spare - 2 * count, part), jnp.float32)], axis=0
    ).astype(jnp.bfloat16)
    latent_ref[rows:, width:] = jnp.zeros((spare, LANES), jnp.bfloat16)
    for send in sends:
        send[:, :width + LANES] = latent_ref[...]
        send[rows:, width + LANES:] = jnp.zeros((spare, part), jnp.bfloat16)


def attention_backward(rank, pieces, weights, keyvalue, key_rope, query_low, query, tokens, scale, tables,
                       w_output, w_keyvalue, w_query):
    rows, model = tokens.shape
    count = len(pieces)
    part = model // count
    wide = query.shape[1]
    kv_width = keyvalue.shape[1]
    sent_rows = pieces[0].shape[0]
    bf16, f32 = jnp.bfloat16, jnp.float32
    sent_width = KV_RANK + LANES
    out_shape = [
        jax.ShapeDtypeStruct(shape, kind)
        for shape, kind in (
            ((rows, model), bf16), ((1, model), f32), ((rows, wide), bf16), ((rows, kv_width), bf16),
            ((rows, part), f32), ((sent_rows, sent_width), bf16),
        ) + (((sent_rows, sent_width + part), bf16),) * (count - 1)
    ]
    inputs = [*pieces, weights, keyvalue, key_rope, query_low, query, tokens, scale, *tables[:3]]
    streamed = [w_output, w_keyvalue, w_query]
    return pl.pallas_call(
        attention_backward_kernel,
        grid_spec=pltpu.PrefetchScalarGridSpec(
            num_scalar_prefetch=1,
            grid=(1,),
            in_specs=full_specs(inputs) + [pl.BlockSpec(memory_space=pl.ANY)] * len(streamed),
            out_specs=full_specs(out_shape),
            scratch_shapes=[pltpu.VMEM(a.shape, a.dtype) for a in streamed]
            + [pltpu.VMEM((rows, wide), f32), pltpu.SemaphoreType.DMA((len(streamed),))],
        ),
        out_shape=out_shape,
        compiler_params=pltpu.CompilerParams(vmem_limit_bytes=48 * 1024 * 1024),
        cost_estimate=pl.CostEstimate(
            flops=4_000_000_000, bytes_accessed=20_000_000, transcendentals=0
        ),
        name="attention_backward",
    )(rank.reshape(1), *inputs, *streamed)


def hidden_kernel(own_ref, token_ref, *rest):
    *pieces, hidden_ref, sent_ref = rest
    value = own_ref[...] + token_ref[...].astype(jnp.float32)
    for piece in pieces:
        value = value + piece[...].astype(jnp.float32)
    hidden_ref[...] = value
    part = value.shape[1]
    total = jnp.sum(value * value, axis=1, keepdims=True)
    high = total.astype(jnp.bfloat16).astype(jnp.float32)
    column = lax.broadcasted_iota(jnp.int32, (value.shape[0], LANES), 1)
    sums = jnp.where(column == 0, high, jnp.where(column == 1, total - high, 0.0))
    sent_ref[:, :part] = value.astype(jnp.bfloat16)
    sent_ref[:, part:] = sums.astype(jnp.bfloat16)


def hidden_rows(own, token_block, pieces):
    tokens, part = own.shape
    return pl.pallas_call(
        hidden_kernel,
        out_shape=[
            jax.ShapeDtypeStruct((tokens, part), jnp.float32),
            jax.ShapeDtypeStruct((tokens, part + LANES), jnp.bfloat16),
        ],
        compiler_params=pltpu.CompilerParams(vmem_limit_bytes=32 * 1024 * 1024),
        name="hidden_rows",
    )(own, token_block, *pieces)


def owner_rows_kernel(first_ref, block_ref, out_ref):
    sources, rows, _ = block_ref.shape
    _, experts, cap, part = out_ref.shape
    line = lax.broadcasted_iota(jnp.int32, (8, LANES), 0)
    column = lax.broadcasted_iota(jnp.int32, (8, LANES), 1)
    select = ((column == line + first_ref[0]) & (line < experts)).astype(jnp.bfloat16)
    earlier = (
        lax.broadcasted_iota(jnp.int32, (rows, rows), 0)
        < lax.broadcasted_iota(jnp.int32, (rows, rows), 1)
    ).astype(jnp.bfloat16)
    slot = lax.broadcasted_iota(jnp.int32, (cap, rows), 0).astype(jnp.float32)
    chosen = jnp.concatenate(
        [matmul_nt(select, block_ref[source, :, part:]) for source in range(sources)], axis=0
    )
    place = matmul(chosen.astype(jnp.bfloat16), earlier)
    for source in range(sources):
        picks = [
            jnp.where((slot == place[line:line + 1]) & (chosen[line:line + 1] > 0.5), 1.0, 0.0)
            for line in range(8 * source, 8 * source + experts)
        ]
        picks = jnp.concatenate(picks, axis=0).astype(jnp.bfloat16)
        out = matmul(picks, block_ref[source, :, :part]).astype(jnp.bfloat16)
        out_ref[source] = out.reshape(experts, cap, part)


def owner_rows(first, gathered, experts, cap):
    groups, rows, wide = gathered.shape
    part = wide - LANES
    step = 8
    return pl.pallas_call(
        owner_rows_kernel,
        grid_spec=pltpu.PrefetchScalarGridSpec(
            num_scalar_prefetch=1,
            grid=(groups // step,),
            in_specs=[pl.BlockSpec((step, rows, wide), lambda i, f: (i, 0, 0))],
            out_specs=pl.BlockSpec((step, experts, cap, part), lambda i, f: (i, 0, 0, 0)),
        ),
        out_shape=jax.ShapeDtypeStruct((groups, experts, cap, part), jnp.bfloat16),
        compiler_params=pltpu.CompilerParams(vmem_limit_bytes=60 * 1024 * 1024),
        cost_estimate=pl.CostEstimate(
            flops=2 * groups * experts * cap * rows * part, bytes_accessed=13_000_000,
            transcendentals=0,
        ),
        name="owner_rows",
    )(first, gathered)


def route_rows_kernel(rank_ref, dispatch_ref, mask_ref, gain_ref, router_ref, *rest):
    pieces, (rows_ref, wide_ref, logit_ref, scale_ref) = rest[:-4], rest[-4:]
    count = len(pieces)
    part = pieces[0].shape[1] - LANES
    model = count * part
    half = LANES // 2

    @pl.when(pl.program_id(0) == 0)
    def _():
        total = sum(jnp.sum(piece[:, part:].astype(jnp.float32), axis=1, keepdims=True)
                    for piece in pieces)
        scale = lax.rsqrt(total / model + EPS)
        scale_ref[...] = scale
        logits = jnp.zeros(logit_ref.shape, jnp.float32)
        for place in range(count):
            turn = lax.rem(rank_ref[0] - place + count, count)
            block = pieces[0][:, :part].astype(jnp.float32)
            for number in range(1, count):
                block = jnp.where(turn == number, pieces[number][:, :part].astype(jnp.float32),
                                  block)
            columns = slice(place * part, (place + 1) * part)
            block = (block * scale * gain_ref[:, columns]).astype(jnp.bfloat16)
            wide_ref[:, columns] = block
            logits += matmul(block, router_ref[columns, :])
        logit_ref[...] = logits
        sigmas = mask_ref[...] / (1.0 + jnp.exp(-logits))
        gates = ROUTE_SCALE * sigmas / jnp.sum(sigmas, axis=1, keepdims=True)
        high = gates.astype(jnp.bfloat16).astype(jnp.float32)
        wide_ref[:, model:] = jnp.concatenate([high, gates - high], axis=1).astype(jnp.bfloat16)

    rows_ref[...] = matmul(dispatch_ref[...], wide_ref[...]).astype(jnp.bfloat16)


def route_rows(rank, dispatch, mask, gain, router, pieces):
    slots, tokens = dispatch.shape
    model, experts = router.shape
    block = 256

    def whole(*shape):
        return pl.BlockSpec(shape, lambda i, r: (0, 0))

    return pl.pallas_call(
        route_rows_kernel,
        grid_spec=pltpu.PrefetchScalarGridSpec(
            num_scalar_prefetch=1,
            grid=(slots // block,),
            in_specs=[
                pl.BlockSpec((block, tokens), lambda i, r: (i, 0)),
                whole(tokens, experts), whole(1, model), whole(model, experts),
            ] + [whole(*piece.shape) for piece in pieces],
            out_specs=[
                pl.BlockSpec((block, model + LANES), lambda i, r: (i, 0)),
                whole(tokens, model + LANES), whole(tokens, experts), whole(tokens, 1),
            ],
        ),
        out_shape=[
            jax.ShapeDtypeStruct((slots, model + LANES), jnp.bfloat16),
            jax.ShapeDtypeStruct((tokens, model + LANES), jnp.bfloat16),
            jax.ShapeDtypeStruct((tokens, experts), jnp.float32),
            jax.ShapeDtypeStruct((tokens, 1), jnp.float32),
        ],
        compiler_params=pltpu.CompilerParams(vmem_limit_bytes=48 * 1024 * 1024),
        cost_estimate=pl.CostEstimate(
            flops=2 * slots * tokens * model, bytes_accessed=13_000_000, transcendentals=0
        ),
        name="route_rows",
    )(rank.reshape(1), dispatch, mask, gain.reshape(1, model), router, *pieces)


def norm_back_kernel(own_ref, extra_ref, pick_ref, back_ref, mask_ref, logit_ref, scale_ref, hidden_ref,
                     gain_ref, router_ref, cotangent_ref, *rest):
    *pieces, grad_ref, sent_ref, logit_grad_ref = rest
    part = own_ref.shape[1]
    rows, experts = mask_ref.shape
    model = part * (len(pieces) + 1)
    gathered = matmul(pick_ref[...], back_ref[...])
    norm_grad = own_ref[...] + gathered[:, :part]
    extra = extra_ref[...].astype(jnp.float32) + gathered[:, part:]
    for piece in pieces:
        norm_grad = norm_grad + piece[:, :part].astype(jnp.float32)
        extra = extra + piece[:, part:].astype(jnp.float32)
    logits = logit_ref[...]
    sigmas = mask_ref[...] / (1.0 + jnp.exp(-logits))
    total = jnp.sum(sigmas, axis=1, keepdims=True)
    gate_grad = extra[:, :experts]
    weighted_sum = jnp.sum(gate_grad * sigmas, axis=1, keepdims=True)
    sigma_grad = ROUTE_SCALE * (gate_grad / total - weighted_sum / (total * total))
    logit_grad = (sigma_grad * sigmas * (1.0 - sigmas)).astype(jnp.bfloat16)
    logit_grad_ref[...] = logit_grad
    norm_grad = norm_grad + matmul_nt(logit_grad, router_ref[...])
    mean = (
        jnp.sum(extra[:, experts:experts + 2], axis=1, keepdims=True)
        + jnp.sum(logit_grad.astype(jnp.float32) * logits, axis=1, keepdims=True)
    ) / model
    scale = scale_ref[...]
    unit = hidden_ref[...] * scale
    gain_grad = jnp.sum(norm_grad * unit, axis=0, keepdims=True)
    grad = cotangent_ref[...].astype(jnp.float32) + scale * (norm_grad * gain_ref[...] - unit * mean)
    grad_ref[...] = grad
    sent_ref[:rows, :] = grad.astype(jnp.bfloat16)
    high = gain_grad.astype(jnp.bfloat16).astype(jnp.float32)
    row = lax.broadcasted_iota(jnp.int32, (sent_ref.shape[0] - rows, part), 0)
    sums = jnp.where(row == 0, high, jnp.where(row == 1, gain_grad - high, 0.0))
    sent_ref[rows:, :] = sums.astype(jnp.bfloat16)


def norm_back(own, extra, pick, back, mask, logits, scale, hidden, gain, router, cotangent, pieces):
    rows, part = own.shape
    bf16, f32 = jnp.bfloat16, jnp.float32
    return pl.pallas_call(
        norm_back_kernel,
        out_shape=[
            jax.ShapeDtypeStruct((rows, part), f32), jax.ShapeDtypeStruct((rows + 16, part), bf16),
            jax.ShapeDtypeStruct(mask.shape, bf16),
        ],
        compiler_params=pltpu.CompilerParams(vmem_limit_bytes=32 * 1024 * 1024),
        cost_estimate=pl.CostEstimate(
            flops=400_000_000, bytes_accessed=5_000_000, transcendentals=rows * 64
        ),
        name="norm_back",
    )(own, extra, pick, back, mask, logits, scale, hidden, gain.reshape(1, part), router, cotangent, *pieces)


def put_pairs(first, grad, row, column, mine_ref, other_ref):
    rows = slice(row, row + grad.shape[2])
    columns = slice(column, column + grad.shape[3])
    even, odd = grad[:, 0], grad[:, 1]
    mine_ref[:, rows, columns] = jnp.where(first, even, odd).astype(jnp.bfloat16)
    other_ref[:, rows, columns] = jnp.where(first, odd, even).astype(jnp.bfloat16)


def late_weights_kernel(core_ref, n_ref, b_ref, t_ref, l_ref, token_ref, w_latent_ref, ffn_ref, query_ref,
                        mixed_ref, logit_ref, kv_ref, latent_ref, latent_gain_ref, cosine_ref, sine_ref,
                        scale_ref, *rest):
    *pieces, latent_grad_ref, mine_ref, other_ref, gain_buf, latent_gain_buf = rest
    step = pl.program_id(0)
    steps = pl.num_programs(0)
    pairs, chunk, _ = mine_ref.shape
    rows = latent_ref.shape[0]
    block = n_ref.shape[1]
    first = core_ref[0] == 0

    @pl.when(step == 0)
    def _():
        total = pieces[0][...].astype(jnp.float32)
        for piece in pieces[1:]:
            total = total + piece[...].astype(jnp.float32)
        count = steps
        for number in range(count):
            gain_buf[number] = (
                total[rows + number:rows + number + 1, :block]
                + total[rows + count + number:rows + count + number + 1, :block]
            )
        latent = latent_ref[...]
        compressed = latent[:, :KV_RANK]
        scale = lax.rsqrt(jnp.mean(compressed * compressed, axis=1, keepdims=True) + EPS)
        unit = compressed * scale
        grad = total[:rows, :KV_RANK]
        gains = jnp.sum(grad * unit, axis=0, keepdims=True)
        width = KV_RANK // count
        for number in range(count):
            latent_gain_buf[number] = gains[:, number * width:(number + 1) * width]
        grad = grad * latent_gain_ref[...]
        grad = scale * (grad - unit * jnp.mean(unit * grad, axis=1, keepdims=True))
        half = ROPE // 2
        former = total[:rows, KV_RANK:KV_RANK + half]
        latter = total[:rows, KV_RANK + half:KV_RANK + ROPE]
        cosine, sine = cosine_ref[...], sine_ref[...]
        latent_grad_ref[...] = jnp.concatenate(
            [grad, former * cosine + latter * sine, latter * cosine - former * sine], axis=1
        ).astype(jnp.bfloat16)

    def by_pairs(grad):
        return grad.reshape(pairs, 2, grad.shape[0] // (2 * pairs), grad.shape[1])

    low = 0
    for rows_ref, grads in (
        (n_ref, query_ref), (b_ref, mixed_ref), (n_ref, latent_grad_ref), (t_ref, logit_ref)
    ):
        grad = matmul_tn(rows_ref[...], grads[...])
        put_pairs(first, by_pairs(grad), 0, low, mine_ref, other_ref)
        low += grad.shape[1]
    grad = by_pairs(matmul_tn(l_ref[...], kv_ref[...]))
    kv_chunk = grad.shape[2]
    columns = grad.shape[3] * kv_chunk // chunk
    for place in range(chunk // kv_chunk):
        put_pairs(first, grad[:, :, :, place * columns:(place + 1) * columns], place * kv_chunk, low,
                  mine_ref, other_ref)
    unit = token_ref[...].astype(jnp.float32) * scale_ref[...]
    routed = matmul(latent_grad_ref[...], w_latent_ref[...])
    gain = gain_buf[step] + jnp.sum(routed * unit, axis=0, keepdims=True)
    line = lax.broadcasted_iota(jnp.int32, (LANES, block), 0)
    gains = by_pairs(jnp.where(line == 0, gain, jnp.where(line == 1, ffn_ref[...], 0.0)).T)
    width = latent_gain_buf.shape[2]
    line = lax.broadcasted_iota(jnp.int32, (LANES, width), 0)
    more = by_pairs(jnp.where(line == 2, latent_gain_buf[step], 0.0).T)
    gains = jnp.concatenate([gains[:, :, :kv_chunk] + more, gains[:, :, kv_chunk:]], axis=2)
    put_pairs(first, gains, 0, low + columns, mine_ref, other_ref)


def late_weights(core, groups, normed, branch, normed_two, latent_normed, tokens, w_latent, ffn_gain, query,
                 mixed, logit, kv, latent, latent_gain, cosine, sine, scale, pieces):
    rows_count, model = normed.shape
    steps = 4
    block = model // steps
    chunk = model // groups
    latent_width = latent.shape[1]
    columns = (
        query.shape[1] + mixed.shape[1] + latent_width + logit.shape[1]
        + kv.shape[1] * latent_normed.shape[1] // model + LANES
    )
    rows = pl.BlockSpec((rows_count, block), lambda i, c: (0, i))

    def whole(array):
        return pl.BlockSpec(array.shape, lambda i, c: (0, 0))

    piece_block = pl.BlockSpec(pieces[0].shape, lambda i, c: (0, 0))
    gain = latent_gain.reshape(1, -1)
    fixed = [query, mixed, logit, kv, latent, gain, cosine, sine, scale]
    return pl.pallas_call(
        late_weights_kernel,
        grid_spec=pltpu.PrefetchScalarGridSpec(
            num_scalar_prefetch=1,
            grid=(steps,),
            in_specs=[
                rows, rows, rows,
                pl.BlockSpec((rows_count, latent_normed.shape[1] // steps), lambda i, c: (0, i)),
                rows, pl.BlockSpec((latent_width, block), lambda i, c: (0, i)),
                pl.BlockSpec((1, block), lambda i, c: (0, i)),
            ] + [whole(array) for array in fixed] + [piece_block] * len(pieces),
            out_specs=[whole(latent)] + [
                pl.BlockSpec((groups // 2 // steps, chunk, columns), lambda i, c: (i, 0, 0))
            ] * 2,
            scratch_shapes=[
                pltpu.VMEM((steps, 1, block), jnp.float32),
                pltpu.VMEM((steps, 1, KV_RANK // steps), jnp.float32),
            ],
        ),
        out_shape=[jax.ShapeDtypeStruct(latent.shape, jnp.bfloat16)]
        + [jax.ShapeDtypeStruct((groups // 2, chunk, columns), jnp.bfloat16)] * 2,
        compiler_params=pltpu.CompilerParams(vmem_limit_bytes=56 * 1024 * 1024),
        cost_estimate=pl.CostEstimate(
            flops=2 * rows_count * model * columns, bytes_accessed=16_000_000, transcendentals=0
        ),
        name="late_weights",
    )(core.reshape(1), normed, branch, normed_two, latent_normed, tokens, w_latent.T, ffn_gain, *fixed,
      *pieces)


def split_kernel(place_ref, mine_ref, got_ref, *outs):
    side = len(outs) // 2
    near = outs[0].shape[1]
    for step in range(side):
        to_z = lax.rem(place_ref[0] + step, side)
        to_x = lax.rem(place_ref[1] + step, side)
        for line in range(side):
            value = mine_ref[line, to_x, :near, :].astype(jnp.float32)
            value = value + got_ref[line, to_x, :near, :].astype(jnp.float32)
            outs[step][line] = value.astype(outs[step].dtype)
            value = mine_ref[to_z, line, near:, :].astype(jnp.float32)
            value = value + got_ref[to_z, line, near:, :].astype(jnp.float32)
            outs[side + step][line] = value.astype(outs[side + step].dtype)


def turn_kernel(place_ref, *refs):
    side = len(refs) // 4
    ins, outs = refs[:2 * side], refs[2 * side:]
    for half in range(2):
        for step in range(side):
            index = lax.rem(place_ref[half] + step, side)
            value = ins[half * side][index]
            for number in range(1, side):
                value = value + ins[half * side + number][index].astype(jnp.float32)
            out = outs[half * side + step]
            out[...] = value.astype(out.dtype)


def whole_call(kernel, place, arrays, shapes, name):
    return pl.pallas_call(
        kernel,
        grid_spec=pltpu.PrefetchScalarGridSpec(
            num_scalar_prefetch=1,
            grid=(1,),
            in_specs=[
                pl.BlockSpec(a.shape, lambda i, p, n=a.ndim: (0,) * n) for a in arrays
            ],
            out_specs=[
                pl.BlockSpec(a.shape, lambda i, p, n=len(a.shape): (0,) * n) for a in shapes
            ],
        ),
        out_shape=shapes,
        compiler_params=pltpu.CompilerParams(vmem_limit_bytes=56 * 1024 * 1024),
        cost_estimate=pl.CostEstimate(
            flops=0, bytes_accessed=sum(2 * a.size for a in arrays) * 2, transcendentals=0
        ),
        name=name,
    )(place, *arrays)


def tree_scatter(mine, other, group, groups):
    side = math.isqrt(groups // 2)
    rows, columns = mine.shape[1:]
    near = rows // 2
    far = rows - near
    place = jnp.stack([group // (2 * side), lax.rem(group // 2, side)])

    def moved(array, move):
        pairs = []
        for index in range(groups):
            z, x, core = index // (2 * side), index // 2 % side, index % 2
            z, x, core = move(z, x, core)
            pairs.append((index, ((z % side) * side + x % side) * 2 + core))
        return lax.ppermute(array, "expert", pairs)

    def shape(*sizes, kind=jnp.bfloat16):
        return jax.ShapeDtypeStruct(sizes, kind)

    got = moved(other, lambda z, x, core: (z, x, 1 - core))
    square = (side, side, rows, columns)
    shapes = [shape(side, n, columns, kind=jnp.float32 if step == 0 else jnp.bfloat16)
              for n in (near, far) for step in range(side)]
    parts = list(whole_call(
        split_kernel, place, [mine.reshape(square), got.reshape(square)], shapes, "split_sum"
    ))
    sent = parts[0]
    for step in range(1, side):
        parts[step] = moved(parts[step], lambda z, x, core: (z, x + step, core))
        parts[side + step] = moved(parts[side + step], lambda z, x, core: (z + step, x, core))
    shapes = [shape(n, columns, kind=jnp.float32 if step == 0 else jnp.bfloat16)
              for n in (near, far) for step in range(side)]
    parts = list(whole_call(turn_kernel, place, parts, shapes, "turn_sum"))
    turned = parts[0]
    for step in range(1, side):
        parts[step] = moved(parts[step], lambda z, x, core: (z + step, x, core))
        parts[side + step] = moved(parts[side + step], lambda z, x, core: (z, x + step, core))
    halves = [
        sum(p.astype(jnp.float32) for p in parts[low:low + side]) for low in (0, side)
    ]
    return (jnp.concatenate(halves, axis=0), sent, turned)


def shards(
    tokens,
    cotangent,
    attn_gain,
    w_query,
    w_latent,
    latent_gain,
    w_keyvalue,
    w_output,
    ffn_gain,
    w_router,
    shared_gate,
    shared_up,
    shared_down,
    expert_gate,
    expert_up,
    expert_down,
    routes,
):
    bf16 = jnp.bfloat16
    f32 = jnp.float32
    tok_rows, model_width = tokens.shape
    top_count = routes.shape[1]
    expert_count = w_router.shape[1]
    local_experts, _, hidden_width = expert_gate.shape
    groups = lax.axis_size("expert")
    ranks = lax.axis_size("tensor")
    rank = lax.axis_index("tensor")
    group = lax.axis_index("expert")
    part = model_width // ranks
    capacity = (4 * tok_rows * top_count + 3 * expert_count - 1) // (3 * expert_count)
    slot_count = expert_count * capacity
    per_group = local_experts * capacity
    qk_width = NOPE + ROPE
    local_heads = w_query.shape[1] // qk_width

    expert_ids = jnp.arange(expert_count, dtype=jnp.int32)
    selector = routes[:, :, None] == expert_ids[None, None, :]
    chosen_mask = jnp.sum(selector.astype(f32), axis=1)

    cotangent_part = column_block(cotangent, rank, part)
    chosen_low = jnp.pad(chosen_mask.astype(bf16), ((0, 0), (0, LANES - expert_count)))
    all_grads = lax.all_gather(
        jnp.concatenate([cotangent_part, chosen_low], axis=1), "expert", axis=0
    )

    tables = rotary_constants(tok_rows, local_heads)
    (normed, scale_one, query_pre, query_low, latent, latent_normed, keyvalue, key_rope, weights_full,
     attn_mixed, attended, *sends) = attention_forward(
        rank, tokens, attn_gain, latent_gain, tables, w_latent, w_query, w_keyvalue, w_output, ranks
    )

    token_ids = jnp.arange(tok_rows, dtype=jnp.int32)
    before = (token_ids[:, None] > token_ids[None, :]).astype(bf16)
    earlier = matmul(before, after(chosen_mask, attended).astype(bf16))
    place = jnp.sum(jnp.where(selector, earlier[:, None, :], 0.0), axis=-1).astype(jnp.int32)
    expert_place = lax.rem(routes, local_experts) * groups + routes // local_experts
    slot_ids = jnp.arange(slot_count, dtype=jnp.int32)

    def one_hot(target, sideways):
        shape = (tok_rows, slot_count) if sideways else (slot_count, tok_rows)
        found = jnp.zeros(shape, jnp.bool_)
        for choice in range(top_count):
            if sideways:
                found = found | (target[:, choice][:, None] == slot_ids[None, :])
            else:
                found = found | (slot_ids[:, None] == target[:, choice][None, :])
        return found.astype(bf16)

    dispatch = one_hot(routes * capacity + place, False)
    combine = one_hot(routes * capacity + place, True)
    by_expert = one_hot(expert_place * capacity + place, True)
    by_expert = by_expert.reshape(tok_rows, local_experts, groups * capacity)

    sends = [shift_ranks(sent, step + 1, ranks) for step, sent in enumerate(sends)]
    hidden_part, sent = hidden_rows(attended, column_block(tokens, rank, part), sends)
    first = (group * local_experts).reshape(1)
    pieces = [sent] + [shift_ranks(sent, step, ranks) for step in range(1, ranks)]

    rows_sent, wide, logits, scale_two = route_rows(
        rank, dispatch, chosen_mask, ffn_gain, w_router, pieces
    )
    normed_two = wide[:, :model_width]
    unit_two_part = hidden_part * scale_two
    sigmas = jax.nn.sigmoid(logits) * chosen_mask
    sigma_total = jnp.sum(sigmas, axis=-1, keepdims=True)
    arrived = lax.all_to_all(
        rows_sent.reshape(groups, per_group, -1), "expert", split_axis=0, concat_axis=0, tiled=True
    )
    grad_quarter = owner_rows(first, after(all_grads, wide), local_experts, capacity)
    grad_arrived = lax.all_gather(grad_quarter, "tensor", axis=0)

    shared_gate_pre = matmul(normed_two, shared_gate)
    shared_up_pre = matmul(normed_two, shared_up)
    shared_act = (jax.nn.silu(shared_gate_pre) * shared_up_pre).astype(bf16)
    shared_part = matmul(shared_act, shared_down).astype(bf16)
    shared_part = lax.psum_scatter(
        shared_part.reshape(tok_rows, ranks, part).transpose(1, 0, 2), "tensor",
        scatter_dimension=0, tiled=True,
    ).reshape(tok_rows, part)
    grad_shared_act = matmul_nt(cotangent, shared_down)
    shared_gate_grad, shared_up_grad = silu_back(grad_shared_act, shared_gate_pre, shared_up_pre)
    norm_part = matmul_nt(shared_gate_grad, shared_gate) + matmul_nt(shared_up_grad, shared_up)
    shared_dot = jnp.sum(
        shared_gate_grad.astype(f32) * shared_gate_pre + shared_up_grad.astype(f32) * shared_up_pre,
        axis=-1, keepdims=True,
    )
    shared_grads = shared_weights(
        normed_two, cotangent, shared_gate_grad, shared_up_grad, shared_act, groups
    )

    width = -(-hidden_width // LANES) * LANES
    widen = ((0, 0), (0, 0), (0, width - hidden_width))
    gate_up = jnp.concatenate([jnp.pad(expert_gate, widen), jnp.pad(expert_up, widen)], axis=2)
    down = jnp.pad(expert_down, ((0, 0), (0, width - hidden_width), (0, 0)))
    gate_up_t = gate_up.transpose(0, 2, 1)
    down_t = down.transpose(0, 2, 1)
    weights = (gate_up, gate_up_t, down, down_t)
    arrived = after(
        arrived, shared_grads, shared_part, norm_part, shared_dot, combine, by_expert, *weights
    ).reshape(groups, local_experts, capacity, -1)
    produced, back, pre_grad, act_weighted = expert_rows(
        0, first, arrived, grad_arrived, weights, True
    )
    back = lax.psum_scatter(back, "tensor", scatter_dimension=0, tiled=True)[0]
    produced, direct, next_grad, next_weighted = expert_rows(
        1, first, arrived, grad_arrived, weights, False, produced
    )
    direct = lax.all_to_all(direct, "expert", split_axis=0, concat_axis=0, tiled=True)
    weight_grads = expert_weights(
        1, arrived, grad_arrived, next_grad, next_weighted, hidden_width
    )
    weight_grads = expert_weights(
        0, arrived, grad_arrived, pre_grad, act_weighted, hidden_width, weight_grads
    )
    direct = after(direct, *weight_grads).reshape(groups * capacity, -1)
    grad_expert_gate, grad_expert_up, grad_expert_down = weight_grads
    produced = lax.psum_scatter(
        produced.reshape(ranks, groups, per_group, part), "tensor", scatter_dimension=0, tiled=True
    )[0]
    back = lax.all_to_all(
        after(back, direct), "expert", split_axis=0, concat_axis=0, tiled=True
    ).reshape(groups * capacity, -1)

    norm_grad, extra_low, *sends = combine_rows(
        rank, by_expert[:, 1], direct, norm_part, shared_dot, ranks
    )
    pieces = [shift_ranks(after(sent, back), step + 1, ranks) for step, sent in enumerate(sends)]
    router_rows = lax.dynamic_slice_in_dim(w_router, rank * part, part, axis=0)
    ffn_gain_part = lax.dynamic_slice_in_dim(ffn_gain, rank * part, part, axis=0)
    hidden_grad, sent, logit_grad = norm_back(
        norm_grad, extra_low, by_expert[:, 0], back, chosen_mask, logits, scale_two, hidden_part,
        ffn_gain_part, router_rows, cotangent_part, pieces,
    )
    pieces = [sent] + [shift_ranks(sent, step, ranks) for step in range(1, ranks)]

    (branch_low, grad_ffn_gain, query_pre_grad, keyvalue_grad, normed_grad, latent_sent,
     *sends) = attention_backward(
        rank, pieces, weights_full, keyvalue, key_rope, query_low, query_pre, tokens, scale_one, tables,
        w_output, w_keyvalue, w_query,
    )
    pieces = [shift_ranks(sent, step + 1, ranks) for step, sent in enumerate(sends)]

    returned = lax.all_to_all(
        after(produced, back, branch_low), "expert", split_axis=0, concat_axis=0, tiled=True
    ).reshape(slot_count, part)

    chunk = model_width // groups
    kv_chunk = KV_RANK // groups
    latent_grad, mine, other = late_weights(
        lax.rem(group, 2), groups, normed, branch_low, normed_two, latent_normed, tokens, w_latent,
        grad_ffn_gain, query_pre_grad, attn_mixed, logit_grad, keyvalue_grad, latent, latent_gain,
        tables[3], tables[4], scale_one, [after(latent_sent, returned)] + pieces,
    )
    late, late_sent, late_turned = tree_scatter(mine, other, group, groups)

    routed_part = matmul(combine, after(returned, late_sent))
    output_part = (hidden_part + shared_part.astype(f32) + routed_part).astype(bf16)
    output = lax.all_gather(output_part, "tensor", axis=0)
    output = output.transpose(1, 0, 2).reshape(tok_rows, model_width)

    sums = latent_sent[:tok_rows, KV_RANK + ROPE:KV_RANK + ROPE + 2].astype(f32)
    for piece in pieces:
        normed_grad = normed_grad + piece[:tok_rows, -part:].astype(f32)
        sums = sums + piece[:tok_rows, KV_RANK + ROPE:KV_RANK + ROPE + 2].astype(f32)
    latent_rows = lax.dynamic_slice_in_dim(w_latent, rank * part, part, axis=0)
    normed_grad = normed_grad + matmul_nt(latent_grad, latent_rows)
    row_mean = (
        jnp.sum(sums, axis=-1, keepdims=True)
        + jnp.sum(latent_grad.astype(f32) * latent, axis=-1, keepdims=True)
    ) / model_width
    unit_one_part = column_block(tokens, rank, part).astype(f32) * scale_one
    attn_gain_part = lax.dynamic_slice_in_dim(attn_gain, rank * part, part, axis=0)
    grad_tokens = hidden_grad + scale_one * (
        normed_grad * attn_gain_part - unit_one_part * row_mean
    )
    grad_tokens = after(grad_tokens.astype(bf16), late_turned)
    grad_tokens, _ = gather_columns(grad_tokens, rank, ranks, part)

    shared_width = shared_gate.shape[1]
    early = lax.psum_scatter(
        after(shared_grads, direct).reshape(groups * 3 * chunk, shared_width), "expert",
        scatter_dimension=0, tiled=True,
    )
    early = after(early, late_turned).astype(f32)
    grad_shared_gate = early[:chunk]
    grad_shared_up = early[chunk:2 * chunk]
    grad_shared_down = early[2 * chunk:].T

    edges = [0]
    for columns in (
        query_pre_grad.shape[1], attn_mixed.shape[1], latent_grad.shape[1], expert_count,
        keyvalue_grad.shape[1] * KV_RANK // model_width, LANES,
    ):
        edges.append(edges[-1] + columns)
    grad_query, grad_output, grad_latent, grad_router, kv_rows, gains = (
        late[:, low:high] for low, high in zip(edges[:-1], edges[1:])
    )
    grad_keyvalue = jnp.concatenate(
        [kv_rows[low:low + kv_chunk] for low in range(0, chunk, kv_chunk)], axis=1
    )
    return (
        output,
        grad_tokens,
        gains[:, 0],
        grad_query,
        grad_latent,
        gains[:kv_chunk, 2],
        grad_keyvalue,
        grad_output.T,
        gains[:, 1],
        grad_router,
        grad_shared_gate,
        grad_shared_up,
        grad_shared_down,
        grad_expert_gate.transpose(0, 2, 1),
        grad_expert_up.transpose(0, 2, 1),
        grad_expert_down,
    )


def solution(mesh):
    return jax.shard_map(
        shards,
        mesh=mesh,
        in_specs=(
            P("expert", None),
            P("expert", None),
            P(),
            P(None, "tensor"),
            P(),
            P(),
            P(None, "tensor"),
            P("tensor", None),
            P(),
            P(),
            P(None, "tensor"),
            P(None, "tensor"),
            P("tensor", None),
            P("expert", None, "tensor"),
            P("expert", None, "tensor"),
            P("expert", "tensor", None),
            P("expert", None),
        ),
        out_specs=(
            P("expert", None),
            P("expert", None),
            P("expert"),
            P("expert", "tensor"),
            P("expert", None),
            P("expert"),
            P("expert", "tensor"),
            P("tensor", "expert"),
            P("expert"),
            P("expert", None),
            P("expert", "tensor"),
            P("expert", "tensor"),
            P("tensor", "expert"),
            P("expert", None, "tensor"),
            P("expert", None, "tensor"),
            P("expert", "tensor", None),
        ),
        check_vma=False,
    )
```

time: 1340 us -> 574 us (0.43)
  waiting for transfers between devices: 795 us -> 223 us
  matrix products: 166 us -> 17.9 us
  Pallas kernels: 0 us -> 138 us
  blocking collectives: 93.9 us -> 0 us
  local copies, waits for them, and re-layouts: 168 us -> 75.4 us
  other arithmetic: 64.7 us -> 25.7 us
  starting transfers between devices: 35.1 us -> 68 us
    reduce_scatter x8 -> x4, waiting for transfers between devices: 402 us -> 0.04 us  [the longest x1 0.02 us: shards(): back = lax.psum_scatter(back, 'tensor', scatter_dimension=0, tiled=True)[0]]
    all_to_all x4, waiting for transfers between devices: 326 us -> 121 us  [the longest x1 61 us: shards(): lax.all_to_all(rows_sent.reshape(groups, per_group, -1), 'expert', split_...]
    pallas_call x0 -> x15, Pallas kernels: none -> 138 us  [the longest x2 40 us: expert_rows(): pl.pallas_call(functools.partial(expert_rows_kernel, sideways), grid_spec...]
    ppermute x0 -> x31, waiting for transfers between devices: none -> 102 us  [the longest x18 68.1 us: shift_ranks(): lax.ppermute(values, 'tensor', [(i, (i + step) % count) for i in range(co...]
    dot_general x15 -> x4, matrix products: 95.9 us -> 8.03 us  [matmul_nt(): lax.dot_general(left_side, right_side, (((1,), (1,)), ((), ())), preferre...]
    gather x4 -> x0, local copies, waits for them, and re-layouts: 72.2 us -> none  [the longest x1 20 us: shards(): outgoing_grad = padded_grad[source].reshape(buffer_shape)]
    psum x3 -> x0, waiting for transfers between devices: 67.4 us -> none  [the longest x1 40.7 us: shards(): lax.psum(matmul(attn_mixed, w_output).astype(jnp.bfloat16), 'tensor')]
    unnamed x1 -> x0, blocking collectives: 65.4 us -> none
  transfers between devices with their start and end apart: 15 -> 42, of which waited for: 13 -> 25; matrix products, arithmetic and copies ran while one was open for 20% -> 14% of each run, Pallas kernels for 0% -> 20%
where the time goes in v1:
time: 574 us; the launch traced here: 563 us
  waiting for transfers between devices  223 us (39%)
  Pallas kernels  138 us (24%)
  local copies, waits for them, and re-layouts  75.4 us (13%)
  starting transfers between devices  68 us (12%)
  other arithmetic  25.7 us (4%)
  matrix products  17.9 us (3%)
  between operations  15.2 us (3%)
    ppermute x18, waiting for transfers between devices, shift_ranks(): lax.ppermute(values, 'tensor', [(i, (i + step) % count) for i in range(co...  68.1 us
    all_to_all x1, waiting for transfers between devices, shards(): lax.all_to_all(rows_sent.reshape(groups, per_group, -1), 'expert', split_...  61 us
    unnamed x156, local copies, waits for them, and re-layouts  40.9 us
    pallas_call x2, Pallas kernels, expert_rows(): pl.pallas_call(functools.partial(expert_rows_kernel, sideways), grid_spec...  40 us
    ppermute x13, waiting for transfers between devices, moved(): return lax.ppermute(array, 'expert', pairs)  33.6 us
    all_to_all x1, waiting for transfers between devices, shards(): lax.all_to_all(direct, 'expert', split_axis=0, concat_axis=0, tiled=True)  27.8 us
    all_to_all x1, waiting for transfers between devices, shards(): lax.all_to_all(after(produced, back, branch_low), 'expert', split_axis=0,...  25.4 us
    pallas_call x2, Pallas kernels, expert_weights(): pl.pallas_call(expert_weights_kernel, grid=(steps,), in_specs=in_specs, o...  24 us
  transfers between devices with their start and end apart: 42, of which 25 were waited for; matrix products, arithmetic and copies ran while one was open for 14% of the time, Pallas kernels for 20%

profile of v1, /device:TPU:0, one launch (start us, length us, event | category | flops | bytes accessed | tf_op | source)
XLA Modules:
  0.0 563.2 jit_solution(5491422812274727451)
XLA Ops:
  15.1 10.3 %attention_forward.1 = (bf16[256,2048]{1,0:T(8,128)(2,1)}, f32[256,1]{1,0:T(8,128)S(1)}, f32[256,768]{1,0:T(8,128)S(1)}, bf16[256,768]{1,0:T(8,128)(2,1)S(1)}, f...) custom-call(s32[1]{0:T(128)} %bitcast.rank_ref, ...), custom_call_target="tpu_custom_call" | custom-call | flops 5000000000 | bytes 16000000 | tf_op jit(solution)/shard_map/attention_forward/pallas_call | solution.py:476
  30.9 1.7 collective-permute-start
  32.5 2.9 collective-permute-start.1
  38.2 2.0 copy.133.router_ref
  40.8 6.6 %collective-permute-done.1.rest_1_ = bf16[256,512]{1,0:T(8,128)(2,1)} collective-permute-done((bf16[256,512]{1,0:T(8,128)(2,1)}, bf16[256,512]{1,0:T(8,128)(2,1)}, u32[]{:S(2)}, u32[]{:S(2)}) %collective-permute-start.1) | collective-permute-done | bytes 262176 | tf_op jit(solution)/shard_map/ppermute | solution.py:72
  49.8 2.2 collective-permute-start.5
  55.2 11.0 %collective-permute-done.5.rest_3_ = bf16[256,640]{1,0:T(8,128)(2,1)S(1)} collective-permute-done((bf16[256,640]{1,0:T(8,128)(2,1)S(1)}, bf16[256,640]{1,0:T(8,128)(2,1)S(1)}, u32[]{:S(2)}, u32[]{:S(2)}) %collective-permute-start.5) | collective-permute-done | bytes 327712 | tf_op jit(solution)/shard_map/ppermute | solution.py:72
  66.2 3.5 collective-permute-done.3.rest_1_
  70.9 7.7 %route_rows.1 = (bf16[2048,2176]{1,0:T(8,128)(2,1)}, bf16[256,2176]{1,0:T(8,128)(2,1)S(1)}, f32[256,64]{1,0:T(8,128)S(1)}, f32[256,1]{1,0:T(8,128)S(1)}) custom-call(s32[1]{0:T(128)} %bitcast.rank_ref, bf16[2048,256]{1,0:T(8,128)(2,1)S(1)} %fusion.8.dispatch_ref, f32[256,64]{1,0:T(8,128)S(1)} %copy.132.mask_ref, f32[1,2048]{1,0:T(1,128)S(1)} %bitcast.75, ...), custom_call_target="tpu_custom_call" | custom-call | flops 2147483648 | bytes 13000000 | tf_op jit(solution)/shard_map/route_rows/pallas_call | solution.py:744
  80.2 7.1 %owner_rows.1 = bf16[32,2,32,512]{3,2,1,0:T(8,128)(2,1)} custom-call(s32[1]{0:T(128)} %bitcast.14.first_ref, bf16[32,256,640]{2,1,0:T(8,128)(2,1)} %bitcast.83), custom_call_target="tpu_custom_call" | custom-call | flops 536870912 | bytes 13000000 | tf_op jit(solution)/shard_map/owner_rows/pallas_call | solution.py:685
  87.4 8.2 %all-to-all-start = ((bf16[32,64,2176]{2,1,0:T(8,128)(2,1)}), bf16[32,64,2176]{2,1,0:T(8,128)(2,1)}, u32[]{:S(2)}, u32[]{:S(2)}) async-start(bf16[32,64,2176]{2,1,0:T(8,128)(2,1)} %bitcast.84), calls=%async_computation.1 | async-start | bytes 17825792 | tf_op jit(solution)/shard_map/all_to_all | solution.py:1130
  95.9 4.8 copy.150
  100.7 5.4 pad_bitcast_fusion
  106.2 4.6 copy.155.wd_ref
  110.8 8.0 %fusion.44 = (bf16[2,768,2048]{2,1,0:T(8,128)(2,1)}, bf16[2,2048,768]{1,2,0:T(8,128)(2,1)}) fusion(bf16[2,2048,352]{1,2,0:T(8,128)(2,1)} %param.36, bf16[2,2048,352]{1,2,0:T(8,128)(2,1)} %param.35), kind=kLoop, calls=%fused_computation.109 | loop fusion | flops 25165824 | bytes 18350080 | tf_op jit(solution)/shard_map/transpose | solution.py:1159
  118.9 8.7 %copy.154.wgu_ref = bf16[2,2048,768]{2,1,0:T(8,128)(2,1)} copy(bf16[2,2048,768]{1,2,0:T(8,128)(2,1)} %get-tuple-element.190) | data formatting | bytes 12582912 | tf_op jit(solution)/shard_map/concatenate | solution.py:1157
  127.6 2.8 or_convert_fusion
  130.4 3.3 fusion.50
  134.9 2.0 add_reduce_fusion
  136.9 7.1 %shared_weights.1 = bf16[32,192,704]{2,1,0:T(8,128)(2,1)} custom-call(bf16[256,2048]{1,0:T(8,128)(2,1)S(1)} %slice.134.n_ref.t_ref, bf16[256,2048]{1,0:T(8,128)(2,1)S(1)} %copy-done.10, bf16[256,704]{1,0:T(8,128)(2,1)S(1)} %get-tuple-element.188.gate_ref, bf16[256,704]{1,0:T(8,128)(2,1)S(1)} %get-tuple-element.187.up_ref, ...), custom_call_target="tpu_custom_call" | custom-call | flops 2214592512 | bytes 14000000 | tf_op jit(solution)/shard_map/shared_weights/pallas_call | solution.py:272
  145.0 2.3 convolution_add_fusion.shared_ref
  147.3 61.0 %all-to-all-done = bf16[32,64,2176]{2,1,0:T(8,128)(2,1)} async-done(((bf16[32,64,2176]{2,1,0:T(8,128)(2,1)}), bf16[32,64,2176]{2,1,0:T(8,128)(2,1)}, u32[]{:S(2)}, u32[]{:S(2)}) %all-to-all-start) | async-done | bytes 8912928 | tf_op jit(solution)/shard_map/all_to_all | solution.py:1130
  208.2 19.7 %expert_rows_0.1 = (bf16[4,32,2,32,512]{4,3,2,1,0:T(8,128)(2,1)}, bf16[4,32,32,640]{3,2,1,0:T(8,128)(2,1)}, bf16[1024,768]{1,0:T(8,128)(2,1)}, bf16[1024,384]{1,0:T(8,128)(2,1)}) custom-call(s32[1]{0:T(128)} %bitcast.14.first_ref, bf16[32,2,32,2176]{3,2,1,0:T(8,128)(2,1)} %bitcast.25.x_ref.gate_ref, bf16[32,2,32,2176]{3,2,1,0:T(8,128)(2,1)} %bitcast.25.x_ref.gate_ref, ...), custom_call_target="tpu_custom_call" | custom-call | flops 9663676416 | bytes 30000000 | tf_op jit(solution)/shard_map/expert_rows_0/pallas_call | solution.py:184
  228.0 20.3 %expert_rows_1.1 = (bf16[4,32,2,32,512]{4,3,2,1,0:T(8,128)(2,1)}, bf16[32,32,2176]{2,1,0:T(8,128)(2,1)}, bf16[1024,768]{1,0:T(8,128)(2,1)}, bf16[1024,384]{1,0:T(8,128)(2,1)}) custom-call(s32[1]{0:T(128)S(6)} %add.145.first_ref, bf16[32,2,32,2176]{3,2,1,0:T(8,128)(2,1)} %bitcast.25.x_ref.gate_ref, ...), custom_call_target="tpu_custom_call", output_to_operand_aliasing={{0}: (8, {})} | custom-call | flops 9663676416 | bytes 30000000 | tf_op jit(solution)/shard_map/expert_rows_1/pallas_call | solution.py:184
  248.3 4.9 all-to-all-start.1
  253.2 2.9 convolution_convert_fusion
  258.0 12.0 %expert_weights_1.1 = (f32[2,352,2048]{2,1,0:T(8,128)}, f32[2,352,2048]{2,1,0:T(8,128)}, f32[2,352,2048]{2,1,0:T(8,128)}) custom-call(bf16[32,2,32,2176]{3,2,1,0:T(8,128)(2,1)} %bitcast.25.x_ref.gate_ref, bf16[4,32,2,32,512]{4,3,2,1,0:T(8,128)(2,1)} %bitcast.79, bf16[1024,768]{1,0:T(8,128)(2,1)} %get-tuple-element.117.dgu_ref, ...), custom_call_target="tpu_custom_call" | custom-call | flops 4831838208 | bytes 22000000 | tf_op jit(solution)/shard_map/expert_weights_1/pallas_call | solution.py:237
  270.1 12.0 %expert_weights_0.1 = (f32[2,352,2048]{2,1,0:T(8,128)}, f32[2,352,2048]{2,1,0:T(8,128)}, f32[2,352,2048]{2,1,0:T(8,128)}) custom-call(bf16[32,2,32,2176]{3,2,1,0:T(8,128)(2,1)} %bitcast.25.x_ref.gate_ref, bf16[4,32,2,32,512]{4,3,2,1,0:T(8,128)(2,1)} %bitcast.80, ...), custom_call_target="tpu_custom_call", output_to_operand_aliasing={{0}: (4, {}), {1}: (5, {}), {2}: (6, {})} | custom-call | flops 4831838208 | bytes 22000000 | tf_op jit(solution)/shard_map/expert_weights_0/pallas_call | solution.py:237
  282.1 27.8 %all-to-all-done.1 = bf16[32,32,2176]{2,1,0:T(8,128)(2,1)} async-done(((bf16[32,32,2176]{2,1,0:T(8,128)(2,1)}), bf16[32,32,2176]{2,1,0:T(8,128)(2,1)}, u32[]{:S(2)}, u32[]{:S(2)}) %all-to-all-start.1) | async-done | bytes 4456480 | tf_op jit(solution)/shard_map/all_to_all | solution.py:1172
  310.0 4.1 all-to-all-start.2
  314.1 2.3 slice_bitcast_fusion
  319.8 4.6 combine_rows.1
  328.1 6.8 %all-to-all-done.2 = bf16[32,32,640]{2,1,0:T(8,128)(2,1)S(1)} async-done(((bf16[32,32,640]{2,1,0:T(8,128)(2,1)}), bf16[32,32,640]{2,1,0:T(8,128)(2,1)S(1)}, u32[]{:S(2)}, u32[]{:S(2)}) %all-to-all-start.2) | async-done | bytes 1310752 | tf_op jit(solution)/shard_map/all_to_all | solution.py:1184
  336.3 1.8 collective-permute-start.8
  339.1 17.0 %collective-permute-done.6.rest_0_ = bf16[256,640]{1,0:T(8,128)(2,1)S(1)} collective-permute-done((bf16[256,640]{1,0:T(8,128)(2,1)}, bf16[256,640]{1,0:T(8,128)(2,1)S(1)}, u32[]{:S(2)}, u32[]{:S(2)}) %collective-permute-start.6) | collective-permute-done | bytes 327712 | tf_op jit(solution)/shard_map/ppermute | solution.py:72
  356.1 9.2 %collective-permute-done.7.rest_1_ = bf16[256,640]{1,0:T(8,128)(2,1)S(1)} collective-permute-done((bf16[256,640]{1,0:T(8,128)(2,1)}, bf16[256,640]{1,0:T(8,128)(2,1)S(1)}, u32[]{:S(2)}, u32[]{:S(2)}) %collective-permute-start.7) | collective-permute-done | bytes 327712 | tf_op jit(solution)/shard_map/ppermute | solution.py:72
  365.3 2.8 collective-permute-done.8.rest_2_
  377.7 1.7 collective-permute-start.10
  379.8 6.9 %collective-permute-done.11.refs_3_ = bf16[272,512]{1,0:T(8,128)(2,1)S(1)} collective-permute-done((bf16[272,512]{1,0:T(8,128)(2,1)S(1)}, bf16[272,512]{1,0:T(8,128)(2,1)S(1)}, u32[]{:S(2)}, u32[]{:S(2)}) %collective-permute-start.11) | collective-permute-done | bytes 278560 | tf_op jit(solution)/shard_map/ppermute | solution.py:72
  388.3 6.7 %collective-permute-done.9.refs_1_ = bf16[272,512]{1,0:T(8,128)(2,1)S(1)} collective-permute-done((bf16[272,512]{1,0:T(8,128)(2,1)S(1)}, bf16[272,512]{1,0:T(8,128)(2,1)S(1)}, u32[]{:S(2)}, u32[]{:S(2)}) %collective-permute-start.9) | collective-permute-done | bytes 278560 | tf_op jit(solution)/shard_map/ppermute | solution.py:72
  397.1 10.2 %attention_backward.1 = (bf16[256,2048]{1,0:T(8,128)(2,1)}, f32[1,2048]{1,0:T(1,128)S(1)}, bf16[256,768]{1,0:T(8,128)(2,1)S(1)}, bf16[256,1024]{1,0:T(8,128)(2,1...) custom-call(s32[1]{0:T(128)} %bitcast.rank_ref, ...), custom_call_target="tpu_custom_call" | custom-call | flops 4000000000 | bytes 20000000 | tf_op jit(solution)/shard_map/attention_backward/pallas_call | solution.py:609
  411.0 4.9 all-to-all-start.3
  416.7 2.8 collective-permute-start.13
  420.5 25.4 %all-to-all-done.3 = bf16[32,64,512]{2,1,0:T(8,128)(2,1)} async-done(((bf16[32,64,512]{2,1,0:T(8,128)(2,1)}), bf16[32,64,512]{2,1,0:T(8,128)(2,1)}, u32[]{:S(2)}, u32[]{:S(2)}) %all-to-all-start.3) | async-done | bytes 2097184 | tf_op jit(solution)/shard_map/all_to_all | solution.py:1207
  447.8 11.4 %late_weights.1 = (bf16[256,576]{1,0:T(8,128)(2,1)}, bf16[16,64,2304]{2,1,0:T(8,128)(2,1)}, bf16[16,64,2304]{2,1,0:T(8,128)(2,1)}) custom-call(s32[1]{0:T(128)} %bitcast.39.core_ref, bf16[256,2048]{1,0:T(8,128)(2,1)} %get-tuple-element.146.n_ref, bf16[256,2048]{1,0:T(8,128)(2,1)} %get-tuple-element.144.b_ref, bf16[256,2048]{1,0:T(8,128)(2,1)} %copy-done.2, ...), custom_call_target="tpu_custom_call" | custom-call | flops 2415919104 | bytes 16000000 | tf_op jit(solution)/shard_map/late_weights/pallas_call | solution.py:922
  462.0 5.6 collective-permute-done.15
  467.5 8.2 %split_sum.1 = (f32[4,32,2304]{2,1,0:T(8,128)}, bf16[4,32,2304]{2,1,0:T(8,128)(2,1)}, bf16[4,32,2304]{2,1,0:T(8,128)(2,1)}, bf16[4,32,2304]{2,1,0:T(8,128)(2,1)}...) custom-call(s32[2]{0:T(128)} %pad_add_fusion.place_ref, ...), custom_call_target="tpu_custom_call" | custom-call | bytes 18874368 | tf_op jit(solution)/shard_map/split_sum/pallas_call | solution.py:981
  475.8 1.8 collective-permute-start.16
  479.2 2.8 collective-permute-start.17
  484.8 2.8 collective-permute-start.20
  487.6 6.7 %collective-permute-done.16.refs_1_ = bf16[4,32,2304]{2,1,0:T(8,128)(2,1)S(1)} collective-permute-done((bf16[4,32,2304]{2,1,0:T(8,128)(2,1)}, bf16[4,32,2304]{2,1,0:T(8,128)(2,1)S(1)}, u32[]{:S(2)}, u32[]{:S(2)}) %collective-permute-start.16) | collective-permute-done | bytes 589856 | tf_op jit(solution)/shard_map/ppermute | solution.py:1015
  494.3 3.0 collective-permute-start.21
  498.9 3.9 add_convert_fusion.1
  502.8 8.3 %collective-permute-done.17.refs_2_ = bf16[4,32,2304]{2,1,0:T(8,128)(2,1)S(1)} collective-permute-done((bf16[4,32,2304]{2,1,0:T(8,128)(2,1)}, bf16[4,32,2304]{2,1,0:T(8,128)(2,1)S(1)}, u32[]{:S(2)}, u32[]{:S(2)}) %collective-permute-start.17) | collective-permute-done | bytes 589856 | tf_op jit(solution)/shard_map/ppermute | solution.py:1015
  512.5 5.3 collective-permute-done.20.refs_6_
  517.8 4.7 turn_sum.1
  522.5 2.7 collective-permute-start.24
  525.6 1.7 fusion.45
  528.3 2.0 collective-permute-start.25
  530.3 1.9 collective-permute-start.26
  536.6 2.2 collective-permute-done.26
  539.0 3.0 collective-permute-start.30
  543.9 1.8 collective-permute-done.29
  553.7 2.3 copy.163
  (255 shorter events, 85.9 us)
Async XLA Ops:
  7.2 127.7 %copy-start = (bf16[2048,704]{0,1:T(8,128)(2,1)S(1)}, bf16[2048,704]{0,1:T(8,128)(2,1)}, u32[]{:S(2)}) copy-start(bf16[2048,704]{0,1:T(8,128)(2,1)} %param.33) | copy-start | bytes 8650756
  7.2 73.0 %all-gather.7.cloned.1.call-start = ((), (), s32[]{:S(2)}) async-start(), calls=%async_computation.12 | async-start | bytes 10813440 | tf_op jit(solution)/shard_map/all_gather | solution.py:1086
  10.7 197.5 %all-gather.9.cloned.1.call-start = ((), (), s32[]{:S(2)}) async-start(), calls=%async_computation.13 | async-start | bytes 10485760 | tf_op jit(solution)/shard_map/all_gather | solution.py:1134
  15.1 21.8 %copy-start.62 = (s32[256,6]{0,1:T(8,128)S(1)}, s32[256,6]{0,1:T(8,128)}, u32[]{:S(2)}) copy-start(s32[256,6]{0,1:T(8,128)} %param.38) | copy-start | bytes 18436
  30.9 364.2 %copy-start.14 = (f32[256,1]{1,0:T(8,128)}, f32[256,1]{1,0:T(8,128)S(1)}, u32[]{:S(2)}) copy-start(f32[256,1]{1,0:T(8,128)S(1)} %get-tuple-element.143.refs_10_.scale_ref) | copy-start | bytes 3076
  30.9 38.9 %copy-start.42 = (f32[2048]{0:T(1024)S(1)}, f32[2048]{0:T(1024)}, u32[]{:S(2)}) copy-start(f32[2048]{0:T(1024)} %param.30) | copy-start | bytes 24580
  30.9 9.9 %collective-permute-start = (bf16[256,512]{1,0:T(8,128)(2,1)}, bf16[256,512]{1,0:T(8,128)(2,1)}, u32[]{:S(2)}, u32[]{:S(2)}) collective-permute-start(bf16[256,512]{1,0:T(8,128)(2,1)} %get-tuple-element.101), channel_id=1, source_target_pairs={{0,1},{1,2},{2,3},{3,0},{4,5},{5,6},{6,7},{7,4},{8,9},{9,10},{10,1... | collective-permute-start | bytes 786440 | tf_op jit(solution)/shard_map/ppermute | solution.py:72
  32.5 14.9 %collective-permute-start.1 = (bf16[256,512]{1,0:T(8,128)(2,1)}, bf16[256,512]{1,0:T(8,128)(2,1)}, u32[]{:S(2)}, u32[]{:S(2)}) collective-permute-start(bf16[256,512]{1,0:T(8,128)(2,1)} %get-tuple-element.102), channel_id=1, source_target_pairs={{0,2},{1,3},{2,0},{3,1},{4,6},{5,7},{6,4},{7,5},{8,10},{9,11},{10,... | collective-permute-start | bytes 786440 | tf_op jit(solution)/shard_map/ppermute | solution.py:72
  35.4 12.0 %collective-permute-start.2 = (bf16[256,512]{1,0:T(8,128)(2,1)}, bf16[256,512]{1,0:T(8,128)(2,1)}, u32[]{:S(2)}, u32[]{:S(2)}) collective-permute-start(bf16[256,512]{1,0:T(8,128)(2,1)} %get-tuple-element.103), channel_id=1, source_target_pairs={{0,3},{1,0},{2,1},{3,2},{4,7},{5,4},{6,5},{7,6},{8,11},{9,8},{10,9... | collective-permute-start | bytes 786440 | tf_op jit(solution)/shard_map/ppermute | solution.py:72
  38.1 40.4 %copy-start.25 = (f32[256,64]{1,0:T(8,128)}, f32[256,64]{1,0:T(8,128)S(1)}, u32[]{:S(2)}) copy-start(f32[256,64]{1,0:T(8,128)S(1)} %copy.132.mask_ref) | copy-start | bytes 196612
  40.8 28.9 %copy-start.63 = (s32[256,1]{0,1:T(1,128)}, s32[256,1]{0,1:T(1,128)S(1)}, u32[]{:S(2)}) copy-start(s32[256,1]{0,1:T(1,128)S(1)} %get-tuple-element.222) | copy-start | bytes 3076
  40.8 28.9 %copy-start.65 = (s32[256,1]{0,1:T(1,128)}, s32[256,1]{0,1:T(1,128)S(1)}, u32[]{:S(2)}) copy-start(s32[256,1]{0,1:T(1,128)S(1)} %get-tuple-element.223) | copy-start | bytes 3076
  40.8 28.9 %copy-start.67 = (s32[256,1]{0,1:T(1,128)}, s32[256,1]{0,1:T(1,128)S(1)}, u32[]{:S(2)}) copy-start(s32[256,1]{0,1:T(1,128)S(1)} %get-tuple-element.224) | copy-start | bytes 3076
  40.8 28.9 %copy-start.69 = (s32[256,1]{0,1:T(1,128)}, s32[256,1]{0,1:T(1,128)S(1)}, u32[]{:S(2)}) copy-start(s32[256,1]{0,1:T(1,128)S(1)} %get-tuple-element.225) | copy-start | bytes 3076
  49.8 19.9 %copy-start.17 = (f32[256,512]{1,0:T(8,128)}, f32[256,512]{1,0:T(8,128)S(1)}, u32[]{:S(2)}) copy-start(f32[256,512]{1,0:T(8,128)S(1)} %get-tuple-element.104.hidden_ref) | copy-start | bytes 1572868
  49.8 16.4 %collective-permute-start.5 = (bf16[256,640]{1,0:T(8,128)(2,1)S(1)}, bf16[256,640]{1,0:T(8,128)(2,1)S(1)}, u32[]{:S(2)}, u32[]{:S(2)}) collective-permute-start(bf16[256,640]{1,0:T(8,128)(2,1)S(1)} %get-tuple-element.106.rest_0_), channel_id=1, source_target_pairs={{0,3},{1,0},{2,1},{3,2},{4,7},{5,4},{6,5},{7,6},{8,11},{9,8},{10,9... | collective-permute-start | bytes 983048 | tf_op jit(solution)/shard_map/ppermute | solution.py:72
  52.0 14.2 %collective-permute-start.4 = (bf16[256,640]{1,0:T(8,128)(2,1)S(1)}, bf16[256,640]{1,0:T(8,128)(2,1)S(1)}, u32[]{:S(2)}, u32[]{:S(2)}) collective-permute-start(bf16[256,640]{1,0:T(8,128)(2,1)S(1)} %get-tuple-element.106.rest_0_), channel_id=1, source_target_pairs={{0,2},{1,3},{2,0},{3,1},{4,6},{5,7},{6,4},{7,5},{8,10},{9,11},{10,... | collective-permute-start | bytes 983048 | tf_op jit(solution)/shard_map/ppermute | solution.py:72
  53.2 16.5 %collective-permute-start.3 = (bf16[256,640]{1,0:T(8,128)(2,1)S(1)}, bf16[256,640]{1,0:T(8,128)(2,1)S(1)}, u32[]{:S(2)}, u32[]{:S(2)}) collective-permute-start(bf16[256,640]{1,0:T(8,128)(2,1)S(1)} %get-tuple-element.106.rest_0_), channel_id=1, source_target_pairs={{0,1},{1,2},{2,3},{3,0},{4,5},{5,6},{6,7},{7,4},{8,9},{9,10},{10,1... | collective-permute-start | bytes 983048 | tf_op jit(solution)/shard_map/ppermute | solution.py:72
  87.4 120.8 %all-to-all-start = ((bf16[32,64,2176]{2,1,0:T(8,128)(2,1)}), bf16[32,64,2176]{2,1,0:T(8,128)(2,1)}, u32[]{:S(2)}, u32[]{:S(2)}) async-start(bf16[32,64,2176]{2,1,0:T(8,128)(2,1)} %bitcast.84), calls=%async_computation.1 | async-start | bytes 17825792 | tf_op jit(solution)/shard_map/all_to_all | solution.py:1130
  95.6 214.3 %reduce-scatter.9.cloned.1.call-start = ((), (), s32[]{:S(2)}) async-start(), calls=%async_computation.10 | async-start | bytes 6553600 | tf_op jit(solution)/shard_map/reduce_scatter | solution.py:1168
  118.8 8.8 %copy-start.74 = (s32[256,1]{0,1:T(1,128)S(1)}, s32[256,1]{0,1:T(1,128)}, u32[]{:S(2)}) copy-start(s32[256,1]{0,1:T(1,128)} %get-tuple-element.211) | copy-start | bytes 3076
  118.8 8.8 %copy-start.75 = (s32[256,1]{0,1:T(1,128)S(1)}, s32[256,1]{0,1:T(1,128)}, u32[]{:S(2)}) copy-start(s32[256,1]{0,1:T(1,128)} %get-tuple-element.212) | copy-start | bytes 3076
  228.0 183.1 %reduce-scatter.7.cloned.1.call-start = ((), (), s32[]{:S(2)}) async-start(), calls=%async_computation.9 | async-start | bytes 10485760 | tf_op jit(solution)/shard_map/reduce_scatter | solution.py:1181
  248.3 61.6 %all-to-all-start.1 = ((bf16[32,32,2176]{2,1,0:T(8,128)(2,1)}), bf16[32,32,2176]{2,1,0:T(8,128)(2,1)}, u32[]{:S(2)}, u32[]{:S(2)}) async-start(bf16[32,32,2176]{2,1,0:T(8,128)(2,1)} %get-tuple-element.114), calls=%async_computation.4 | async-start | bytes 8912896 | tf_op jit(solution)/shard_map/all_to_all | solution.py:1172
  253.2 245.6 %reduce-scatter.5.cloned.1.call-start = ((), (), s32[]{:S(2)}) async-start(), calls=%async_computation.8 | async-start | bytes 1310720 | tf_op jit(solution)/shard_map/reduce_scatter | solution.py:1140
  258.0 267.6 %reduce-scatter.11.cloned.1.call-start = ((), (), s32[]{:S(2)}) async-start(), calls=%async_computation.11 | async-start | bytes 9732096 | tf_op jit(solution)/shard_map/reduce_scatter | solution.py:1244
  310.0 24.9 %all-to-all-start.2 = ((bf16[32,32,640]{2,1,0:T(8,128)(2,1)}), bf16[32,32,640]{2,1,0:T(8,128)(2,1)S(1)}, u32[]{:S(2)}, u32[]{:S(2)}) async-start(bf16[32,32,640]{2,1,0:T(8,128)(2,1)} %bitcast.93), calls=%async_computation.5 | async-start | bytes 2621440 | tf_op jit(solution)/shard_map/all_to_all | solution.py:1184
  328.1 67.0 %copy-start.56 = (bf16[256,64]{1,0:T(8,128)(2,1)S(1)}, bf16[256,64]{1,0:T(8,128)(2,1)}, u32[]{:S(2)}) copy-start(bf16[256,64]{1,0:T(8,128)(2,1)} %copy-done.55) | copy-start | bytes 98308
  334.9 21.2 %collective-permute-start.6 = (bf16[256,640]{1,0:T(8,128)(2,1)}, bf16[256,640]{1,0:T(8,128)(2,1)S(1)}, u32[]{:S(2)}, u32[]{:S(2)}) collective-permute-start(bf16[256,640]{1,0:T(8,128)(2,1)} %copy-done.48), channel_id=1, source_target_pairs={{0,1},{1,2},{2,3},{3,0},{4,5},{5,6},{6,7},{7,4},{8,9},{9,10},{10,1... | collective-permute-start | bytes 983048 | tf_op jit(solution)/shard_map/ppermute | solution.py:72
  334.9 30.4 %collective-permute-start.7 = (bf16[256,640]{1,0:T(8,128)(2,1)}, bf16[256,640]{1,0:T(8,128)(2,1)S(1)}, u32[]{:S(2)}, u32[]{:S(2)}) collective-permute-start(bf16[256,640]{1,0:T(8,128)(2,1)} %copy-done.47), channel_id=1, source_target_pairs={{0,2},{1,3},{2,0},{3,1},{4,6},{5,7},{6,4},{7,5},{8,10},{9,11},{10,... | collective-permute-start | bytes 983048 | tf_op jit(solution)/shard_map/ppermute | solution.py:72
  336.3 31.8 %collective-permute-start.8 = (bf16[256,640]{1,0:T(8,128)(2,1)}, bf16[256,640]{1,0:T(8,128)(2,1)S(1)}, u32[]{:S(2)}, u32[]{:S(2)}) collective-permute-start(bf16[256,640]{1,0:T(8,128)(2,1)} %copy-done.46), channel_id=1, source_target_pairs={{0,3},{1,0},{2,1},{3,2},{4,7},{5,4},{6,5},{7,6},{8,11},{9,8},{10,9... | collective-permute-start | bytes 983048 | tf_op jit(solution)/shard_map/ppermute | solution.py:72
  377.7 9.0 %collective-permute-start.11 = (bf16[272,512]{1,0:T(8,128)(2,1)S(1)}, bf16[272,512]{1,0:T(8,128)(2,1)S(1)}, u32[]{:S(2)}, u32[]{:S(2)}) collective-permute-start(bf16[272,512]{1,0:T(8,128)(2,1)S(1)} %get-tuple-element.137.refs_0_), channel_id=1, source_target_pairs={{0,3},{1,0},{2,1},{3,2},{4,7},{5,4},{6,5},{7,6},{8,11},{9,8},{10,9... | collective-permute-start | bytes 835592 | tf_op jit(solution)/shard_map/ppermute | solution.py:72
  377.7 10.6 %collective-permute-start.10 = (bf16[272,512]{1,0:T(8,128)(2,1)S(1)}, bf16[272,512]{1,0:T(8,128)(2,1)S(1)}, u32[]{:S(2)}, u32[]{:S(2)}) collective-permute-start(bf16[272,512]{1,0:T(8,128)(2,1)S(1)} %get-tuple-element.137.refs_0_), channel_id=1, source_target_pairs={{0,2},{1,3},{2,0},{3,1},{4,6},{5,7},{6,4},{7,5},{8,10},{9,11},{10,... | collective-permute-start | bytes 835592 | tf_op jit(solution)/shard_map/ppermute | solution.py:72
  379.4 15.7 %collective-permute-start.9 = (bf16[272,512]{1,0:T(8,128)(2,1)S(1)}, bf16[272,512]{1,0:T(8,128)(2,1)S(1)}, u32[]{:S(2)}, u32[]{:S(2)}) collective-permute-start(bf16[272,512]{1,0:T(8,128)(2,1)S(1)} %get-tuple-element.137.refs_0_), channel_id=1, source_target_pairs={{0,1},{1,2},{2,3},{3,0},{4,5},{5,6},{6,7},{7,4},{8,9},{9,10},{10,1... | collective-permute-start | bytes 835592 | tf_op jit(solution)/shard_map/ppermute | solution.py:72
  411.0 34.9 %all-to-all-start.3 = ((bf16[32,64,512]{2,1,0:T(8,128)(2,1)}), bf16[32,64,512]{2,1,0:T(8,128)(2,1)}, u32[]{:S(2)}, u32[]{:S(2)}) async-start(bf16[32,64,512]{2,1,0:T(8,128)(2,1)} %bitcast.92), calls=%async_computation.6 | async-start | bytes 4194304 | tf_op jit(solution)/shard_map/all_to_all | solution.py:1207
  415.9 137.7 %all-gather.11.cloned.1.call-start = ((), (), s32[]{:S(2)}) async-start(), calls=%async_computation.14 | async-start | bytes 1310720 | tf_op jit(solution)/shard_map/all_gather | solution.py:1222
  416.0 29.9 %collective-permute-start.12 = (bf16[272,1152]{1,0:T(8,128)(2,1)S(1)}, bf16[272,1152]{1,0:T(8,128)(2,1)}, u32[]{:S(2)}, u32[]{:S(2)}) collective-permute-start(bf16[272,1152]{1,0:T(8,128)(2,1)S(1)} %copy-done.45), channel_id=1, source_target_pairs={{0,1},{1,2},{2,3},{3,0},{4,5},{5,6},{6,7},{7,4},{8,9},{9,10},{10,1... | collective-permute-start | bytes 1880072 | tf_op jit(solution)/shard_map/ppermute | solution.py:72
  416.7 30.6 %collective-permute-start.13 = (bf16[272,1152]{1,0:T(8,128)(2,1)S(1)}, bf16[272,1152]{1,0:T(8,128)(2,1)}, u32[]{:S(2)}, u32[]{:S(2)}) collective-permute-start(bf16[272,1152]{1,0:T(8,128)(2,1)S(1)} %get-tuple-element.157), channel_id=1, source_target_pairs={{0,2},{1,3},{2,0},{3,1},{4,6},{5,7},{6,4},{7,5},{8,10},{9,11},{10,... | collective-permute-start | bytes 1880072 | tf_op jit(solution)/shard_map/ppermute | solution.py:72
  419.5 28.3 %collective-permute-start.14 = (bf16[272,1152]{1,0:T(8,128)(2,1)S(1)}, bf16[272,1152]{1,0:T(8,128)(2,1)}, u32[]{:S(2)}, u32[]{:S(2)}) collective-permute-start(bf16[272,1152]{1,0:T(8,128)(2,1)S(1)} %get-tuple-element.158), channel_id=1, source_target_pairs={{0,3},{1,0},{2,1},{3,2},{4,7},{5,4},{6,5},{7,6},{8,11},{9,8},{10,9... | collective-permute-start | bytes 1880072 | tf_op jit(solution)/shard_map/ppermute | solution.py:72
  447.8 12.3 %copy-start.15 = (f32[256,1]{1,0:T(8,128)S(1)}, f32[256,1]{1,0:T(8,128)}, u32[]{:S(2)}) copy-start(f32[256,1]{1,0:T(8,128)} %copy-done.14) | copy-start | bytes 3076
  459.2 8.3 %collective-permute-start.15 = (bf16[16,64,2304]{2,1,0:T(8,128)(2,1)}, bf16[16,64,2304]{2,1,0:T(8,128)(2,1)}, u32[]{:S(2)}, u32[]{:S(2)}) collective-permute-start(bf16[16,64,2304]{2,1,0:T(8,128)(2,1)} %get-tuple-element.160), channel_id=1, source_target_pairs={{0,4},{4,0},{8,12},{12,8},{16,20},{20,16},{24,28},{28,24},{32,36},... | collective-permute-start | bytes 14155784 | tf_op jit(solution)/shard_map/ppermute | solution.py:1015
  467.5 10.1 %copy-start.5 = (f32[256,576]{1,0:T(8,128)S(1)}, f32[256,576]{1,0:T(8,128)}, u32[]{:S(2)}) copy-start(f32[256,576]{1,0:T(8,128)} %copy-done.4) | copy-start | bytes 1769476
  467.5 10.1 %copy-start.58 = (bf16[256,576]{1,0:T(8,128)(2,1)S(1)}, bf16[256,576]{1,0:T(8,128)(2,1)}, u32[]{:S(2)}) copy-start(bf16[256,576]{1,0:T(8,128)(2,1)} %get-tuple-element.165) | copy-start | bytes 884740
  475.8 23.0 %copy-start.19 = (f32[256,512]{1,0:T(8,128)S(1)}, f32[256,512]{1,0:T(8,128)}, u32[]{:S(2)}) copy-start(f32[256,512]{1,0:T(8,128)} %copy-done.17) | copy-start | bytes 1572868
  475.8 23.0 %copy-start.64 = (s32[256,1]{0,1:T(1,128)S(1)}, s32[256,1]{0,1:T(1,128)}, u32[]{:S(2)}) copy-start(s32[256,1]{0,1:T(1,128)} %copy-done.63) | copy-start | bytes 3076
  475.8 23.1 %copy-start.66 = (s32[256,1]{0,1:T(1,128)S(1)}, s32[256,1]{0,1:T(1,128)}, u32[]{:S(2)}) copy-start(s32[256,1]{0,1:T(1,128)} %copy-done.65) | copy-start | bytes 3076
  475.8 23.1 %copy-start.68 = (s32[256,1]{0,1:T(1,128)S(1)}, s32[256,1]{0,1:T(1,128)}, u32[]{:S(2)}) copy-start(s32[256,1]{0,1:T(1,128)} %copy-done.67) | copy-start | bytes 3076
  475.8 23.1 %copy-start.70 = (s32[256,1]{0,1:T(1,128)S(1)}, s32[256,1]{0,1:T(1,128)}, u32[]{:S(2)}) copy-start(s32[256,1]{0,1:T(1,128)} %copy-done.69) | copy-start | bytes 3076
  475.8 18.5 %collective-permute-start.16 = (bf16[4,32,2304]{2,1,0:T(8,128)(2,1)}, bf16[4,32,2304]{2,1,0:T(8,128)(2,1)S(1)}, u32[]{:S(2)}, u32[]{:S(2)}) collective-permute-start(bf16[4,32,2304]{2,1,0:T(8,128)(2,1)} %get-tuple-element.166), channel_id=1, source_target_pairs={{0,8},{4,12},{8,16},{12,20},{16,24},{20,28},{24,0},{28,4},{32,40},... | collective-permute-start | bytes 1769480 | tf_op jit(solution)/shard_map/ppermute | solution.py:1015
  479.2 31.9 %collective-permute-start.17 = (bf16[4,32,2304]{2,1,0:T(8,128)(2,1)}, bf16[4,32,2304]{2,1,0:T(8,128)(2,1)S(1)}, u32[]{:S(2)}, u32[]{:S(2)}) collective-permute-start(bf16[4,32,2304]{2,1,0:T(8,128)(2,1)} %get-tuple-element.167), channel_id=1, source_target_pairs={{0,16},{4,20},{8,24},{12,28},{16,0},{20,4},{24,8},{28,12},{32,48},... | collective-permute-start | bytes 1769480 | tf_op jit(solution)/shard_map/ppermute | solution.py:1015
  482.0 30.5 %collective-permute-start.18 = (bf16[4,32,2304]{2,1,0:T(8,128)(2,1)}, bf16[4,32,2304]{2,1,0:T(8,128)(2,1)}, u32[]{:S(2)}, u32[]{:S(2)}) collective-permute-start(bf16[4,32,2304]{2,1,0:T(8,128)(2,1)} %get-tuple-element.168), channel_id=1, source_target_pairs={{0,24},{4,28},{8,0},{12,4},{16,8},{20,12},{24,16},{28,20},{32,56},... | collective-permute-start | bytes 1769480 | tf_op jit(solution)/shard_map/ppermute | solution.py:1015
  483.4 29.1 %collective-permute-start.19 = (bf16[4,32,2304]{2,1,0:T(8,128)(2,1)}, bf16[4,32,2304]{2,1,0:T(8,128)(2,1)}, u32[]{:S(2)}, u32[]{:S(2)}) collective-permute-start(bf16[4,32,2304]{2,1,0:T(8,128)(2,1)} %get-tuple-element.170), channel_id=1, source_target_pairs={{0,32},{4,36},{8,40},{12,44},{16,48},{20,52},{24,56},{28,60},{32,6... | collective-permute-start | bytes 1769480 | tf_op jit(solution)/shard_map/ppermute | solution.py:1015
  484.8 32.9 %collective-permute-start.20 = (bf16[4,32,2304]{2,1,0:T(8,128)(2,1)}, bf16[4,32,2304]{2,1,0:T(8,128)(2,1)}, u32[]{:S(2)}, u32[]{:S(2)}) collective-permute-start(bf16[4,32,2304]{2,1,0:T(8,128)(2,1)} %get-tuple-element.171), channel_id=1, source_target_pairs={{0,64},{4,68},{8,72},{12,76},{16,80},{20,84},{24,88},{28,92},{32,9... | collective-permute-start | bytes 1769480 | tf_op jit(solution)/shard_map/ppermute | solution.py:1015
  494.3 23.5 %collective-permute-start.21 = (bf16[4,32,2304]{2,1,0:T(8,128)(2,1)}, bf16[4,32,2304]{2,1,0:T(8,128)(2,1)}, u32[]{:S(2)}, u32[]{:S(2)}) collective-permute-start(bf16[4,32,2304]{2,1,0:T(8,128)(2,1)} %get-tuple-element.172), channel_id=1, source_target_pairs={{0,96},{4,100},{8,104},{12,108},{16,112},{20,116},{24,120},{28,124... | collective-permute-start | bytes 1769480 | tf_op jit(solution)/shard_map/ppermute | solution.py:1015
  522.5 23.2 %copy-start.61 = (f32[32,2304]{1,0:T(8,128)S(1)}, f32[32,2304]{1,0:T(8,128)}, u32[]{:S(2)}) copy-start(f32[32,2304]{1,0:T(8,128)} %get-tuple-element.178) | copy-start | bytes 884740
  522.5 28.0 %collective-permute-start.24 = (bf16[256,512]{1,0:T(8,128)(2,1)S(1)}, bf16[256,512]{1,0:T(8,128)(2,1)S(1)}, u32[]{:S(2)}, u32[]{:S(2)}) collective-permute-start(bf16[256,512]{1,0:T(8,128)(2,1)S(1)} %add_convert_fusion), channel_id=1, source_target_pairs={{0,3},{1,0},{2,1},{3,2},{4,7},{5,4},{6,5},{7,6},{8,11},{9,8},{10,9... | collective-permute-start | bytes 786440 | tf_op jit(solution)/shard_map/ppermute | solution.py:72
  525.2 25.3 %collective-permute-start.23 = (bf16[256,512]{1,0:T(8,128)(2,1)S(1)}, bf16[256,512]{1,0:T(8,128)(2,1)}, u32[]{:S(2)}, u32[]{:S(2)}) collective-permute-start(bf16[256,512]{1,0:T(8,128)(2,1)S(1)} %add_convert_fusion), channel_id=1, source_target_pairs={{0,2},{1,3},{2,0},{3,1},{4,6},{5,7},{6,4},{7,5},{8,10},{9,11},{10,... | collective-permute-start | bytes 786440 | tf_op jit(solution)/shard_map/ppermute | solution.py:72
  528.3 7.5 %collective-permute-start.25 = (bf16[32,2304]{1,0:T(8,128)(2,1)}, bf16[32,2304]{1,0:T(8,128)(2,1)S(1)}, u32[]{:S(2)}, u32[]{:S(2)}) collective-permute-start(bf16[32,2304]{1,0:T(8,128)(2,1)} %get-tuple-element.175), channel_id=1, source_target_pairs={{0,32},{4,36},{8,40},{12,44},{16,48},{20,52},{24,56},{28,60},{32,6... | collective-permute-start | bytes 442376 | tf_op jit(solution)/shard_map/ppermute | solution.py:1015
  530.3 8.5 %collective-permute-start.26 = (bf16[32,2304]{1,0:T(8,128)(2,1)}, bf16[32,2304]{1,0:T(8,128)(2,1)S(1)}, u32[]{:S(2)}, u32[]{:S(2)}) collective-permute-start(bf16[32,2304]{1,0:T(8,128)(2,1)} %get-tuple-element.176), channel_id=1, source_target_pairs={{0,64},{4,68},{8,72},{12,76},{16,80},{20,84},{24,88},{28,92},{32,9... | collective-permute-start | bytes 442376 | tf_op jit(solution)/shard_map/ppermute | solution.py:1015
  532.2 6.8 %collective-permute-start.27 = (bf16[32,2304]{1,0:T(8,128)(2,1)}, bf16[32,2304]{1,0:T(8,128)(2,1)S(1)}, u32[]{:S(2)}, u32[]{:S(2)}) collective-permute-start(bf16[32,2304]{1,0:T(8,128)(2,1)} %get-tuple-element.177), channel_id=1, source_target_pairs={{0,96},{4,100},{8,104},{12,108},{16,112},{20,116},{24,120},{28,124... | collective-permute-start | bytes 442376 | tf_op jit(solution)/shard_map/ppermute | solution.py:1015
  535.8 8.1 %collective-permute-start.28 = (bf16[32,2304]{1,0:T(8,128)(2,1)}, bf16[32,2304]{1,0:T(8,128)(2,1)S(1)}, u32[]{:S(2)}, u32[]{:S(2)}) collective-permute-start(bf16[32,2304]{1,0:T(8,128)(2,1)} %get-tuple-element.179), channel_id=1, source_target_pairs={{0,8},{4,12},{8,16},{12,20},{16,24},{20,28},{24,0},{28,4},{32,40},... | collective-permute-start | bytes 442376 | tf_op jit(solution)/shard_map/ppermute | solution.py:1015
  538.8 6.9 %collective-permute-start.29 = (bf16[32,2304]{1,0:T(8,128)(2,1)}, bf16[32,2304]{1,0:T(8,128)(2,1)S(1)}, u32[]{:S(2)}, u32[]{:S(2)}) collective-permute-start(bf16[32,2304]{1,0:T(8,128)(2,1)} %get-tuple-element.180), channel_id=1, source_target_pairs={{0,16},{4,20},{8,24},{12,28},{16,0},{20,4},{24,8},{28,12},{32,48},... | collective-permute-start | bytes 442376 | tf_op jit(solution)/shard_map/ppermute | solution.py:1015
  539.0 6.7 %collective-permute-start.30 = (bf16[32,2304]{1,0:T(8,128)(2,1)}, bf16[32,2304]{1,0:T(8,128)(2,1)S(1)}, u32[]{:S(2)}, u32[]{:S(2)}) collective-permute-start(bf16[32,2304]{1,0:T(8,128)(2,1)} %get-tuple-element.181), channel_id=1, source_target_pairs={{0,24},{4,28},{8,0},{12,4},{16,8},{20,12},{24,16},{28,20},{32,56},... | collective-permute-start | bytes 442376 | tf_op jit(solution)/shard_map/ppermute | solution.py:1015
  543.9 7.6 %collective-permute-start.22 = (bf16[256,512]{1,0:T(8,128)(2,1)S(1)}, bf16[256,512]{1,0:T(8,128)(2,1)S(1)}, u32[]{:S(2)}, u32[]{:S(2)}) collective-permute-start(bf16[256,512]{1,0:T(8,128)(2,1)S(1)} %add_convert_fusion), channel_id=1, source_target_pairs={{0,1},{1,2},{2,3},{3,0},{4,5},{5,6},{6,7},{7,4},{8,9},{9,10},{10,1... | collective-permute-start | bytes 786440 | tf_op jit(solution)/shard_map/ppermute | solution.py:72
  (55 other events, 128.5 us)
Sparse Core Ops, SparseCore 0:
  10.9 60.3 all-gather.6
  87.5 83.0 all-gather.8
  228.1 50.0 reduce-scatter.8
  280.5 94.2 reduce-scatter.6
  377.0 24.7 reduce-scatter.4
  405.9 107.0 reduce-scatter.10
  514.7 30.1 all-gather.10
